TPU v7x, 32 devices: a whole 2x2x4 slice. The times are simulated.
32 devices in a mesh: dp: 8 (over z, y), seq: 4 (over x, core).
Axes of the slice: x: 2, y: 2, z: 4, core: 2. Of those that a mesh axis runs over, the one named last changes fastest.
Arguments:
- tokens: bfloat16 [16, 1024, 1536], P('dp', 'seq'), may hold values from -8 to 8
- segment_ids: int32 [16, 1024], P('dp'), may hold values from 0 to 32, as said below
- w_in: bfloat16 [1536, 6448], P('dp'), may hold values from -0.15625 to 0.15625
- w_out: bfloat16 [3072, 1536], P('dp'), may hold values from -0.109375 to 0.109375
- conv_weight: bfloat16 [3328, 4], P('dp'), may hold values from -3 to 3
- conv_bias: bfloat16 [3328], P('dp'), may hold values from -1.75 to 1.75
- norm_gain: bfloat16 [1536], P('dp'), may hold values from 0.5 to 1.5
- gated_gain: bfloat16 [3072], P('dp'), may hold values from 0.5 to 1.5
- dt_bias: float32 [48], replicated, may hold values from -7 to -2.5
- a_log: float32 [48], replicated, may hold values from 0 to 2.77
- skip_weight: float32 [48], replicated, may hold values from 0.5 to 1.5
- cotangent: bfloat16 [16, 1024, 1536], P('dp', 'seq'), may hold values from -6 to 6
Outputs:
- out: bfloat16 [16, 1024, 1536], P('dp', 'seq')
- tokens_grad: float32 [16, 1024, 1536], P('dp', 'seq')
- w_in_grad: float32 [1536, 6448], P('dp')
- w_out_grad: float32 [3072, 1536], P('dp')
- conv_weight_grad: float32 [3328, 4], P('dp')
- conv_bias_grad: float32 [3328], P('dp')
- norm_gain_grad: float32 [1536], P('dp')
- gated_gain_grad: float32 [3072], P('dp')
- dt_bias_grad: float32 [48], replicated
- a_log_grad: float32 [48], replicated
- skip_weight_grad: float32 [48], replicated
Inputs may be any that keep to these rules, and one draw needn't show every extreme that they name: `segment_ids`: each row starts at 0 and rises by 0 or 1 from one token to the next; in each aligned group of 2 rows one row, which one varies, is a single document.
All inputs are finite; a program needn't handle non-finite values.
Results may differ from a plain program's by a relative error of at most 0.015.
Values may be sent and summed in bfloat16 or wider, within the bound.
A program may use at most 256 MiB of HBM per device.

v0:
```python
from functools import partial

import jax
import jax.numpy as jnp
from jax import lax
from jax.sharding import PartitionSpec as P

SPAN = 256


EPSILON = 1e-05
PRECISE = lax.Precision.HIGHEST


def conv_reset(inputs, kernel, offsets, segment):
    length = inputs.shape[0]
    tap_count = kernel.shape[1]
    summed = inputs * kernel[:, tap_count - 1] + offsets
    for distance in range(1, tap_count):
        earlier = jnp.pad(inputs, ((distance, 0), (0, 0)))[:length]
        earlier_seg = jnp.pad(segment, (distance, 0), constant_values=-1)[:length]
        keeper = (earlier_seg == segment).astype(jnp.float32)
        summed = summed + earlier * keeper[:, None] * kernel[:, tap_count - 1 - distance]
    return jax.nn.silu(summed)


def span_step(decay_rate, head_count, carried_in, pieces):
    memory, seg_before = carried_in
    flat_values, b_block, c_block, deltas, seg_block = pieces
    width_q = seg_block.shape[0]
    values = flat_values.reshape(width_q, head_count, -1)
    log_decay = jnp.cumsum(deltas * decay_rate[:, None], axis=1)
    row_ids = lax.broadcasted_iota(jnp.int32, (width_q, width_q), 0)
    col_ids = lax.broadcasted_iota(jnp.int32, (width_q, width_q), 1)
    linked = (row_ids >= col_ids) & (seg_block[:, None] == seg_block[None, :])
    spread = jnp.where(linked[None, :, :], log_decay[:, :, None] - log_decay[:, None, :], -jnp.inf)
    scores = jnp.dot(c_block, b_block.T, precision=PRECISE)
    weights = jnp.exp(spread) * scores[None, :, :]
    driven = values * deltas.T[:, :, None]
    within = jnp.einsum("hij,jhp->ihp", weights, driven, precision=PRECISE)
    entering = (seg_block == seg_before).astype(jnp.float32)
    carried = (
        jnp.einsum("in,hpn->ihp", c_block, memory, precision=PRECISE)
        * (jnp.exp(log_decay).T * entering[:, None])[:, :, None]
    )
    seg_final = seg_block[width_q - 1]
    leaving = jnp.exp(
        jnp.where(
            (seg_block == seg_final)[None, :],
            log_decay[:, width_q - 1][:, None] - log_decay,
            -jnp.inf,
        )
    )
    kept_share = jnp.exp(log_decay[:, width_q - 1]) * (seg_final == seg_before).astype(jnp.float32)
    memory = memory * kept_share[:, None, None] + jnp.einsum(
        "jhp,jn->hpn", driven * leaving.T[:, :, None], b_block, precision=PRECISE
    )
    return ((memory, seg_final), (within + carried).reshape(width_q, flat_values.shape[1]))


def ssd_scan(values, b_rows, c_rows, deltas, decay_rate, segment):
    length, head_count, head_size = values.shape
    state_size = b_rows.shape[1]
    span_count = length // SPAN
    pieces = (
        values.reshape(span_count, SPAN, head_count * head_size),
        b_rows.reshape(span_count, SPAN, state_size),
        c_rows.reshape(span_count, SPAN, state_size),
        deltas.reshape(span_count, SPAN, head_count).transpose(0, 2, 1),
        segment.reshape(span_count, SPAN),
    )
    initial = (
        jnp.zeros((head_count, head_size, state_size), jnp.float32),
        jnp.array(-1, jnp.int32),
    )
    final_state, outputs = lax.scan(
        jax.checkpoint(partial(span_step, decay_rate, head_count)), initial, pieces
    )
    return outputs.reshape(length, head_count, head_size)


def mixer(
    gate_in,
    conv_in,
    dt_raw,
    bc_raw,
    segment,
    x_kernel,
    x_offsets,
    bc_kernel,
    bc_offsets,
    dt_bias,
    a_log,
    skip_weight,
):
    length, head_count, head_size = conv_in.shape
    values = conv_reset(
        conv_in.reshape(length, head_count * head_size), x_kernel, x_offsets, segment
    ).reshape(length, head_count, head_size)
    bc_rows = conv_reset(bc_raw, bc_kernel, bc_offsets, segment)
    state_size = bc_rows.shape[1] // 2
    deltas = jax.nn.softplus(dt_raw + dt_bias)
    decay_rate = -jnp.exp(a_log)
    gated_out = (
        ssd_scan(
            values, bc_rows[:, :state_size], bc_rows[:, state_size:], deltas, decay_rate, segment
        )
        + skip_weight[:, None] * values
    )
    return gated_out * jax.nn.silu(gate_in)


def local(
    tokens,
    segment_ids,
    w_in,
    w_out,
    conv_weight,
    conv_bias,
    norm_gain,
    gated_gain,
    dt_bias,
    a_log,
    skip_weight,
    cotangent,
):
    groups = lax.axis_size("seq")
    position = lax.axis_index("seq")
    seq_count, shard_len, model_width = tokens.shape
    w_in_all, w_out_all, conv_all, conv_bias_all, norm_all, gated_all = (
        lax.all_gather(w_in, "dp", axis=0, tiled=True),
        lax.all_gather(w_out, "dp", axis=0, tiled=True),
        lax.all_gather(conv_weight, "dp", axis=0, tiled=True),
        lax.all_gather(conv_bias, "dp", axis=0, tiled=True),
        lax.all_gather(norm_gain, "dp", axis=0, tiled=True),
        lax.all_gather(gated_gain, "dp", axis=0, tiled=True),
    )
    inner_width = w_out_all.shape[0]
    head_count = dt_bias.shape[0]
    head_size = inner_width // head_count
    bc_width = w_in_all.shape[1] - 2 * inner_width - head_count
    local_heads = head_count // groups
    first_head = position * local_heads
    local_width = local_heads * head_size
    first_channel = first_head * head_size
    floats = tokens.astype(jnp.float32)
    inverse = lax.rsqrt(jnp.mean(floats * floats, axis=-1, keepdims=True) + EPSILON)
    unit_rows = floats * inverse
    norm_floats = norm_all.astype(jnp.float32)
    normed = (unit_rows * norm_floats).astype(jnp.bfloat16)
    projected = jnp.einsum(
        "std,de->ste", normed, w_in_all, preferred_element_type=jnp.float32
    ).astype(jnp.bfloat16)
    head_cols = projected[:, :, : 2 * inner_width].reshape(
        seq_count, shard_len, head_count, 2 * head_size
    )
    bc_cols = projected[:, :, 2 * inner_width : 2 * inner_width + bc_width]
    dt_cols = projected[:, :, 2 * inner_width + bc_width :]
    head_in, dt_in = (
        lax.all_to_all(head_cols, "seq", split_axis=2, concat_axis=1, tiled=True),
        lax.all_to_all(dt_cols, "seq", split_axis=2, concat_axis=1, tiled=True),
    )
    bc_in = lax.all_gather(bc_cols, "seq", axis=1, tiled=True)
    checked = jax.checkpoint(mixer)

    def local_mix(head_vals, dt_vals, bc_vals, kernel, offsets, bias_all, log_all, skip_all):
        x_kernel = lax.dynamic_slice_in_dim(kernel, first_channel, local_width, 0)
        x_offsets = lax.dynamic_slice_in_dim(offsets, first_channel, local_width, 0)
        dt_local = lax.dynamic_slice_in_dim(bias_all, first_head, local_heads, 0)
        log_local = lax.dynamic_slice_in_dim(log_all, first_head, local_heads, 0)
        skip_local = lax.dynamic_slice_in_dim(skip_all, first_head, local_heads, 0)

        def one_row(heads_row, dt_row, bc_row, seg_row):
            return checked(
                heads_row[:, :, :head_size],
                heads_row[:, :, head_size:],
                dt_row,
                bc_row,
                seg_row,
                x_kernel,
                x_offsets,
                kernel[inner_width:],
                offsets[inner_width:],
                dt_local,
                log_local,
                skip_local,
            )

        return jax.vmap(one_row)(head_vals, dt_vals, bc_vals, segment_ids)

    gated_vals, pullback = jax.vjp(
        local_mix,
        head_in.astype(jnp.float32),
        dt_in.astype(jnp.float32),
        bc_in.astype(jnp.float32),
        conv_all.astype(jnp.float32),
        conv_bias_all.astype(jnp.float32),
        dt_bias,
        a_log,
        skip_weight,
    )
    square_sums = jnp.sum(gated_vals * gated_vals, axis=(2, 3))
    totals = lax.psum(square_sums, "seq")
    norm_root = lax.rsqrt(totals / inner_width + EPSILON)[:, :, None, None]
    gain_local = (
        lax.dynamic_slice_in_dim(gated_all, first_channel, local_width, 0)
        .astype(jnp.float32)
        .reshape(local_heads, head_size)
    )
    scaled = (gated_vals * norm_root * gain_local).astype(jnp.bfloat16)
    returned = lax.all_to_all(scaled, "seq", split_axis=1, concat_axis=2, tiled=True)
    flattened = returned.reshape(seq_count, shard_len, inner_width)
    result = (
        floats + jnp.einsum("stc,cd->std", flattened, w_out_all, preferred_element_type=jnp.float32)
    ).astype(jnp.bfloat16)
    w_out_grad = jnp.einsum("stc,std->cd", flattened, cotangent, preferred_element_type=jnp.float32)
    scaled_grad = jnp.einsum(
        "std,cd->stc", cotangent, w_out_all, preferred_element_type=jnp.float32
    ).astype(jnp.bfloat16)
    scaled_grad = scaled_grad.reshape(seq_count, shard_len, head_count, head_size)
    head_grad = lax.all_to_all(scaled_grad, "seq", split_axis=2, concat_axis=1, tiled=True).astype(
        jnp.float32
    )
    weighted = head_grad * gain_local
    cross = lax.psum(jnp.sum(weighted * gated_vals, axis=(2, 3)), "seq")
    gated_grad = (
        norm_root * weighted - gated_vals * norm_root**3 * (cross / inner_width)[:, :, None, None]
    )
    gain_part = jnp.sum(head_grad * gated_vals * norm_root, axis=(0, 1)).reshape(local_width)
    gated_gain_grad = lax.dynamic_update_slice_in_dim(
        jnp.zeros((inner_width,), jnp.float32), gain_part, first_channel, 0
    )
    head_part, dt_part, bc_part, conv_grad, conv_bias_grad, dt_bias_part, a_log_part, skip_part = (
        pullback(gated_grad)
    )
    back_heads, back_dt = (
        lax.all_to_all(
            head_part.astype(jnp.bfloat16), "seq", split_axis=1, concat_axis=2, tiled=True
        ),
        lax.all_to_all(
            dt_part.astype(jnp.bfloat16), "seq", split_axis=1, concat_axis=2, tiled=True
        ),
    )
    bc_grad = lax.psum_scatter(bc_part.astype(jnp.bfloat16), "seq", scatter_dimension=1, tiled=True)
    projected_grad = jnp.concatenate(
        [back_heads.reshape(seq_count, shard_len, 2 * inner_width), bc_grad, back_dt], axis=-1
    )
    w_in_grad = jnp.einsum(
        "std,ste->de", normed, projected_grad, preferred_element_type=jnp.float32
    )
    normed_grad = jnp.einsum(
        "ste,de->std", projected_grad, w_in_all, preferred_element_type=jnp.float32
    )
    norm_gain_grad = jnp.sum(normed_grad * unit_rows, axis=(0, 1))
    unit_grad = normed_grad * norm_floats
    tokens_grad = cotangent.astype(jnp.float32) + inverse * (
        unit_grad - unit_rows * jnp.mean(unit_grad * unit_rows, axis=-1, keepdims=True)
    )
    gradients = (w_in_grad, w_out_grad, conv_grad, conv_bias_grad, norm_gain_grad, gated_gain_grad)
    pieces = (
        lax.psum_scatter(
            gradients[0].astype(jnp.bfloat16), "dp", scatter_dimension=0, tiled=True
        ).astype(jnp.float32),
        lax.psum_scatter(
            gradients[1].astype(jnp.bfloat16), "dp", scatter_dimension=0, tiled=True
        ).astype(jnp.float32),
        lax.psum_scatter(
            gradients[2].astype(jnp.bfloat16), "dp", scatter_dimension=0, tiled=True
        ).astype(jnp.float32),
        lax.psum_scatter(
            gradients[3].astype(jnp.bfloat16), "dp", scatter_dimension=0, tiled=True
        ).astype(jnp.float32),
        lax.psum_scatter(
            gradients[4].astype(jnp.bfloat16), "dp", scatter_dimension=0, tiled=True
        ).astype(jnp.float32),
        lax.psum_scatter(
            gradients[5].astype(jnp.bfloat16), "dp", scatter_dimension=0, tiled=True
        ).astype(jnp.float32),
    )
    owned = (
        lax.psum(pieces[0].astype(jnp.bfloat16), "seq").astype(jnp.float32),
        lax.psum(pieces[1].astype(jnp.bfloat16), "seq").astype(jnp.float32),
        lax.psum(pieces[2].astype(jnp.bfloat16), "seq").astype(jnp.float32),
        lax.psum(pieces[3].astype(jnp.bfloat16), "seq").astype(jnp.float32),
        lax.psum(pieces[4].astype(jnp.bfloat16), "seq").astype(jnp.float32),
        lax.psum(pieces[5].astype(jnp.bfloat16), "seq").astype(jnp.float32),
    )
    head_sums = lax.psum((dt_bias_part, a_log_part, skip_part), ("dp", "seq"))
    return (
        result,
        tokens_grad,
        owned[0],
        owned[1],
        owned[2],
        owned[3],
        owned[4],
        owned[5],
        head_sums[0],
        head_sums[1],
        head_sums[2],
    )


def solution(mesh):
    return jax.shard_map(
        local,
        mesh=mesh,
        in_specs=(
            P("dp", "seq", None),
            P("dp", None),
            P("dp", None),
            P("dp", None),
            P("dp", None),
            P("dp"),
            P("dp"),
            P("dp"),
            P(),
            P(),
            P(),
            P("dp", "seq", None),
        ),
        out_specs=(
            P("dp", "seq", None),
            P("dp", "seq", None),
            P("dp", None),
            P("dp", None),
            P("dp", None),
            P("dp"),
            P("dp"),
            P("dp"),
            P(),
            P(),
            P(),
        ),
        check_vma=False,
    )
```

profile of v0, /device:TPU:3, one launch (start us, length us, event | category | flops | bytes accessed | tf_op | source)
XLA Modules:
  0.0 2334.9 jit_solution(8796203691906921040)
XLA Ops:
  8.7 140.5 %all-gather.10.cloned.1.call-done = bf16[3072,1536]{1,0:T(8,128)(2,1)} async-done(((bf16[384,1536]{1,0:T(8,128)(2,1)}), bf16[3072,1536]{1,0:T(8,128)(2,1)}) %all-gather.10.cloned.1.call-update) | async-done | bytes 9437200 | tf_op jit(solution)/shard_map/all_gather | solution.py:132
  170.8 41.1 %all-reduce.47 = (bf16[1536]{0:T(1024)(128)(2,1)S(1)}, bf16[3328]{0:T(1024)(128)(2,1)S(1)}) all-reduce(bf16[1536]{0:T(1024)(128)(2,1)S(1)} %dynamic-update-slice.2, bf16[3328]{0:T(1024)(128)(2,1)S(1)} %dynamic-update-slice.3), channel_id=1, replica_groups=mesh['dp'=8,'seq'=4] {'dp'}, use_global_device_ids=true, to_apply=%add.40 | all-reduce | flops 4864 | bytes 19456
  213.7 321.4 %all-gather.6.cloned.1.call-done = bf16[1536,6448]{1,0:T(8,128)(2,1)} async-done(((bf16[192,6448]{1,0:T(8,128)(2,1)}), bf16[1536,6448]{1,0:T(8,128)(2,1)}) %all-gather.6.cloned.1.call-update) | async-done | bytes 19808272 | tf_op jit(solution)/shard_map/all_gather | solution.py:131
  535.1 17.7 fusion.129
  578.6 24.1 %all-gather = bf16[8,416,4]{1,2,0:T(4,128)(2,1)S(1)} all-gather(bf16[1,416,4]{1,2,0:T(4,128)(2,1)S(1)} %bitcast.596), channel_id=1, replica_groups=mesh['dp'=8,'seq'=4] {'dp'}, dimensions={0}, use_global_device_ids=true | all-gather | bytes 29952 | tf_op jit(solution)/shard_map/all_gather | solution.py:133
  604.1 21.3 all-gather.1
  642.7 12.1 all-gather.8.cloned.1.call-done
  673.0 10.7 copy.685
  683.7 12.4 slice.312
  705.9 13.9 divide_multiply_fusion
  730.0 101.3 %while.60 = (s32[]{:T(128)}, f32[2,12,64,128]{3,2,1,0:T(8,128)}, s32[2]{0:T(128)S(1)}, f32[4,2,256,768]{2,3,1,0:T(8,128)}, f32[4,2,256,768]{3,2,0,1:T(8,128)}, /...) while((s32[]{:T(128)}, f32[2,12,64,128]{3,2,1,0:T(8,128)}, ...), condition=%wide.region_4.5_spmd.clone, body=%wide.region_1.4_spmd.clone.sunk | while | flops 2625660416 | bytes 25584260 | solution.py:76
  868.2 22.8 multiply_reduce_fusion.8
  914.0 16.9 multiply_subtract_fusion
  932.0 12.7 copy.826
  969.9 16.1 fusion.153
  1012.0 100.0 %while.61 = (s32[]{:T(128)}, f32[2,12,64,128]{3,2,1,0:T(8,128)S(1)}, s32[2]{0:T(128)S(1)}, f32[4,2,256,768]{2,3,1,0:T(8,128)}, f32[4,2,12,64,128]{4,3,2,1,0:T(8,...) while((s32[]{:T(128)}, ...), condition=%wide.region_12.13_spmd.clone, body=%wide.region_9.12_spmd.clone.sunk | while | flops 2626053632 | bytes 21381816 | solution.py:76
  1149.0 28.2 %multiply_reduce_fusion.6 = (f32[12]{0:T(128)}, f32[2,1024,12,64]{3,1,2,0:T(8,128)}, f32[2,1024,12,64]{3,1,2,0:T(8,128)}) fusion(f32[2,1024,12,64]{3,1,2,0:T(8,128)} %copy.725, f32[2,1024,12,64]{3,1,2,0:T(8,128)} %get-tuple-element.529, f32[2,1024,12,64]{3,1,2,0:T(8,128)} %get-tuple-element.530, f32[2,1024,12,64]{3,1,2,0:T(8,128)} %copy.726, ...), kind=kLoop, calls=%fused_computation.203 | loop fusion | flops 25165812 | bytes 37748832 | tf_op jit(solution)/shard_map/transpose(jvp(vmap(jvp(vmap()))))/checkpoint/reduce_sum | solution.py:108
  1201.2 391.7 %while.62 = (s32[]{:T(128)}, f32[12]{0:T(128)}, f32[2,12,64,128]{3,2,1,0:T(8,128)}, f32[4,2,256,768]{2,3,1,0:T(8,128)}, f32[4,2,256,128]{3,2,1,0:T(8,128)}, /*in...) while((s32[]{:T(128)}, f32[12]{0:T(128)}, ...), condition=%wide.region_27.28_spmd.clone, body=%wide.region_13.27_spmd.clone.sunk | while | flops 6067584512 | bytes 59513860 | solution.py:76
  1327.6 10.7 fusion.339
  1524.1 10.7 fusion.339
  1637.6 13.9 multiply_add_fusion
  1661.2 17.1 fusion.211
  1687.3 14.9 copy.751
  1752.8 36.7 %copy.727 = bf16[2,1024,12,128]{3,0,2,1:T(2,128)(2,1)} copy(bf16[2,1024,12,128]{3,1,2,0:T(8,128)(2,1)S(1)} %add_convert_fusion) | data formatting | bytes 12582912 | tf_op jit(solution)/shard_map/convert_element_type | solution.py:238
  1797.1 66.8 %all-to-all-done.4 = bf16[2,1024,12,128]{3,0,2,1:T(2,128)(2,1)} async-done(((bf16[2,1024,12,128]{3,0,2,1:T(2,128)(2,1)}), bf16[2,1024,12,128]{3,0,2,1:T(2,128)(2,1)}, u32[]{:S(2)}, u32[]{:S(2)}) %all-to-all-start.4) | async-done | bytes 6291488 | tf_op jit(solution)/shard_map/all_to_all | solution.py:237
  1879.9 17.5 bitcast_convert_fusion
  1900.4 42.8 %all-reduce.45 = (f32[48]{0:T(128)}, f32[48]{0:T(128)}, f32[48]{0:T(128)}) all-reduce(f32[48]{0:T(128)S(1)} %dynamic_update_slice.80, f32[48]{0:T(128)S(1)} %multiply_dynamic-update-slice_fusion, f32[48]{0:T(128)S(1)} %dynamic_update_slice.82), channel_id=1, replica_groups=mesh['dp'=8,'seq'=4] {'dp','seq'}, use_global_device_ids=true, to_apply=%region_55.56 | all-reduce | flops 144 | bytes 1152 | tf_op jit(solution)/shard_map/psum | solution.py:288
  1954.6 288.6 %reduce-scatter.9.cloned.1.call-done = bf16[192,6448]{1,0:T(8,128)(2,1)} async-done(((bf16[1536,6448]{1,0:T(8,128)(2,1)}), bf16[192,6448]{1,0:T(8,128)(2,1)}) %reduce-scatter.9.cloned.1.call-update) | async-done | bytes 2476048 | tf_op jit(solution)/shard_map/reduce_scatter | solution.py:261
  2243.2 18.4 fusion.168
  2261.6 28.2 %all-reduce.46 = (bf16[3328]{0:T(1024)(128)(2,1)S(1)}, bf16[1536]{0:T(1024)(128)(2,1)S(1)}, bf16[3072]{0:T(1024)(128)(2,1)S(1)}) all-reduce(bf16[3328]{0:T(1024)(128)(2,1)S(1)} %convert_element_type.258, bf16[1536]{0:T(1024)(128)(2,1)S(1)} %get-tuple-element.973, ...), channel_id=6, replica_groups=mesh['dp'=8,'seq'=4] {'dp'}, use_global_device_ids=true, to_apply=%region_46.47.clone | all-reduce | flops 7936 | bytes 31744
  2290.0 12.8 all-reduce.48
  2309.7 12.1 all-reduce.52.cloned.1.call-done
  (926 shorter events, 1010.5 us)
Async XLA Ops:
  7.2 141.9 %all-gather.10.cloned.1.call-start = ((), (), s32[]{:S(2)}) async-start(), calls=%async_computation.12 | async-start | bytes 10616832 | tf_op jit(solution)/shard_map/all_gather | solution.py:132
  7.9 527.2 %all-gather.6.cloned.1.call-start = ((), (), s32[]{:S(2)}) async-start(), calls=%async_computation.10 | async-start | bytes 22560768 | tf_op jit(solution)/shard_map/all_gather | solution.py:131
  163.5 390.8 %all-to-all-start.3 = ((bf16[2,256,48,64]{1,3,0,2:T(8,128)(2,1)}), bf16[2,256,48,64]{1,3,0,2:T(8,128)(2,1)S(1)}, u32[]{:S(2)}, u32[]{:S(2)}) async-start(bf16[2,256,48,64]{1,3,0,2:T(8,128)(2,1)} %copy.703), calls=%async_computation.3 | async-start | bytes 6291456 | tf_op jit(solution)/shard_map/all_to_all | solution.py:221
  211.9 340.9 %copy-start.37 = (f32[1536]{0:T(1024)}, f32[1536]{0:T(1024)S(1)}, u32[]{:S(2)}) copy-start(f32[1536]{0:T(1024)S(1)} %convert_element_type.220) | copy-start | bytes 18436
  213.7 339.1 %copy-start.52 = (f32[2,256]{1,0:T(2,128)}, f32[2,256]{1,0:T(2,128)S(1)}, u32[]{:S(2)}) copy-start(f32[2,256]{1,0:T(2,128)S(1)} %add_rsqrt_fusion.1) | copy-start | bytes 6148
  554.3 18.8 all-to-all-start.1
  573.0 31.0 %copy-start.69 = (f32[48]{0:T(128)S(1)}, f32[48]{0:T(128)}, u32[]{:S(2)}) copy-start(f32[48]{0:T(128)} %param.28) | copy-start | bytes 580
  573.0 31.1 %copy-start.63 = (bf16[384]{0:T(512)(128)(2,1)S(1)}, bf16[384]{0:T(512)(128)(2,1)}, u32[]{:S(2)}) copy-start(bf16[384]{0:T(512)(128)(2,1)} %param.25) | copy-start | bytes 2308
  573.0 54.4 %copy-start.65 = (f32[48]{0:T(128)S(1)}, f32[48]{0:T(128)}, u32[]{:S(2)}) copy-start(f32[48]{0:T(128)} %param.27) | copy-start | bytes 580
  573.0 90.5 %all-to-all-start = ((bf16[2,256,48,128]{3,1,0,2:T(8,128)(2,1)}), bf16[2,256,48,128]{3,1,0,2:T(8,128)(2,1)}, u32[]{:S(2)}, u32[]{:S(2)}) async-start(bf16[2,256,48,128]{3,1,0,2:T(8,128)(2,1)} %copy.683), calls=%async_computation | async-start | bytes 12582912 | tf_op jit(solution)/shard_map/all_to_all | solution.py:160
  578.4 76.3 %all-gather.8.cloned.1.call-start = ((), (), s32[]{:S(2)}) async-start(), calls=%async_computation.11 | async-start | bytes 1310720 | tf_op jit(solution)/shard_map/all_gather | solution.py:163
  602.8 53.5 %copy-start.50 = (f32[256]{0:T(256)}, f32[256]{0:T(256)S(1)}, u32[]{:S(2)}) copy-start(f32[256]{0:T(256)S(1)} %slice.315) | copy-start | bytes 3076
  604.0 353.8 %copy-start.56 = (f32[12]{0:T(128)}, f32[12]{0:T(128)S(1)}, u32[]{:S(2)}) copy-start(f32[12]{0:T(128)S(1)} %dynamic_slice.138) | copy-start | bytes 148
  604.1 544.9 %copy-start.54 = (f32[12]{0:T(128)}, f32[12]{0:T(128)S(1)}, u32[]{:S(2)}) copy-start(f32[12]{0:T(128)S(1)} %dynamic_slice.140) | copy-start | bytes 148
  642.3 315.5 %copy-start.15 = (f32[4,12,1,2,256]{4,3,0,2,1:T(2,128)}, f32[4,12,1,2,256]{4,3,0,2,1:T(2,128)S(1)}, u32[]{:S(2)}) copy-start(f32[4,12,1,2,256]{4,3,0,2,1:T(2,128)S(1)} %copy.818) | copy-start | bytes 294916
  932.0 67.5 %copy-start.19 = (f32[2,1024]{1,0:T(2,128)}, f32[2,1024]{1,0:T(2,128)S(1)}, u32[]{:S(2)}) copy-start(f32[2,1024]{1,0:T(2,128)S(1)} %get-tuple-element.1133) | copy-start | bytes 24580
  932.0 67.5 %copy-start.21 = (f32[2,1024]{1,0:T(2,128)}, f32[2,1024]{1,0:T(2,128)S(1)}, u32[]{:S(2)}) copy-start(f32[2,1024]{1,0:T(2,128)S(1)} %get-tuple-element.1134) | copy-start | bytes 24580
  932.0 67.5 %copy-start.23 = (f32[2,1024]{1,0:T(2,128)}, f32[2,1024]{1,0:T(2,128)S(1)}, u32[]{:S(2)}) copy-start(f32[2,1024]{1,0:T(2,128)S(1)} %get-tuple-element.1135) | copy-start | bytes 24580
  952.5 727.2 %all-to-all-start.2 = ((bf16[4,2,196608]{2,1,0:T(2,128)(2,1)}), bf16[4,2,196608]{2,1,0:T(2,128)(2,1)}, u32[]{:S(2)}, u32[]{:S(2)}) async-start(bf16[4,2,196608]{2,1,0:T(2,128)(2,1)} %reshape.806), calls=%async_computation.2 | async-start | bytes 6291456 | tf_op jit(solution)/shard_map/all_to_all | solution.py:211
  957.8 922.0 %reduce-scatter.7.cloned.1.call-start = ((), (), s32[]{:S(2)}) async-start(), calls=%async_computation.13 | async-start | bytes 1310720 | tf_op jit(solution)/shard_map/reduce_scatter | solution.py:244
  1203.5 40.9 %copy-start.41 = (s32[2]{0:T(128)}, s32[2]{0:T(128)S(1)}, u32[]{:S(2)}) copy-start(s32[2]{0:T(128)S(1)} %fusion.337) | copy-start | bytes 28 | tf_op jit(solution)/shard_map/transpose(jvp(vmap(jvp(vmap()))))/checkpoint/while
  1299.9 42.0 %copy-start.41 = (s32[2]{0:T(128)}, s32[2]{0:T(128)S(1)}, u32[]{:S(2)}) copy-start(s32[2]{0:T(128)S(1)} %fusion.337) | copy-start | bytes 28 | tf_op jit(solution)/shard_map/transpose(jvp(vmap(jvp(vmap()))))/checkpoint/while
  1398.2 42.0 %copy-start.41 = (s32[2]{0:T(128)}, s32[2]{0:T(128)S(1)}, u32[]{:S(2)}) copy-start(s32[2]{0:T(128)S(1)} %fusion.337) | copy-start | bytes 28 | tf_op jit(solution)/shard_map/transpose(jvp(vmap(jvp(vmap()))))/checkpoint/while
  1496.4 42.0 %copy-start.41 = (s32[2]{0:T(128)}, s32[2]{0:T(128)S(1)}, u32[]{:S(2)}) copy-start(s32[2]{0:T(128)S(1)} %fusion.337) | copy-start | bytes 28 | tf_op jit(solution)/shard_map/transpose(jvp(vmap(jvp(vmap()))))/checkpoint/while
  1610.0 333.2 %reduce-scatter.13.cloned.1.call-start = ((), (), s32[]{:S(2)}) async-start(), calls=%async_computation.16 | async-start | bytes 958464
  1679.7 274.9 %reduce-scatter.11.cloned.1.call-start = ((), (), s32[]{:S(2)}) async-start(), calls=%async_computation.15 | async-start | bytes 10616832 | tf_op jit(solution)/shard_map/reduce_scatter | solution.py:264
  1715.5 74.0 %all-to-all-start.5 = ((bf16[4,2,3072]{2,1,0:T(2,128)(2,1)}), bf16[4,2,3072]{2,1,0:T(2,128)(2,1)S(1)}, u32[]{:S(2)}, u32[]{:S(2)}) async-start(bf16[4,2,3072]{2,1,0:T(2,128)(2,1)} %reshape.808), calls=%async_computation.6 | async-start | bytes 98304 | tf_op jit(solution)/shard_map/all_to_all | solution.py:240
  1789.5 74.3 %all-to-all-start.4 = ((bf16[2,1024,12,128]{3,0,2,1:T(2,128)(2,1)}), bf16[2,1024,12,128]{3,0,2,1:T(2,128)(2,1)}, u32[]{:S(2)}, u32[]{:S(2)}) async-start(bf16[2,1024,12,128]{3,0,2,1:T(2,128)(2,1)} %copy.727), calls=%async_computation.4 | async-start | bytes 12582912 | tf_op jit(solution)/shard_map/all_to_all | solution.py:237
  1794.9 448.3 %reduce-scatter.9.cloned.1.call-start = ((), (), s32[]{:S(2)}) async-start(), calls=%async_computation.14 | async-start | bytes 22560768 | tf_op jit(solution)/shard_map/reduce_scatter | solution.py:261
  1897.4 424.3 %all-reduce.52.cloned.1.call-start = ((), (), s32[]{:S(2)}) async-start(), calls=%async_computation.17 | async-start | bytes 7372800 | tf_op jit(solution)/shard_map/psum | solution.py:281
  1944.2 299.1 %copy-start.66 = (bf16[2,256,256]{1,2,0:T(8,128)(2,1)S(1)}, bf16[2,256,256]{1,2,0:T(8,128)(2,1)}, u32[]{:S(2)}) copy-start(bf16[2,256,256]{1,2,0:T(8,128)(2,1)} %reduce-scatter.7.cloned.1.call-done) | copy-start | bytes 786436
  2243.2 62.0 %copy-start.13 = (bf16[2,256,1536]{2,1,0:T(8,128)(2,1)S(1)}, bf16[2,256,1536]{2,1,0:T(8,128)(2,1)}, u32[]{:S(2)}) copy-start(bf16[2,256,1536]{2,1,0:T(8,128)(2,1)} %param.29) | copy-start | bytes 4718596
  (79 other events, 750.3 us)
Sparse Core Ops, SparseCore 0:
  10.2 138.8 all-gather.9
  150.6 384.3 all-gather.5
  627.5 27.1 all-gather.7
  1610.1 23.5 reduce-scatter.6
  1679.8 60.9 reduce-scatter.12
  1744.2 163.9 reduce-scatter.10
  1912.1 331.0 reduce-scatter.8
  2245.6 76.0 all-reduce.51
where the time goes:
time: 2360 us; the launch traced here: 2330 us
  waiting for transfers between devices  843 us (36%)
  local copies, waits for them, and re-layouts  579 us (25%)
  matrix products  355 us (15%)
  other arithmetic  324 us (14%)
  blocking collectives  183 us (8%)
  starting transfers between devices  29 us (1%)
    all_gather x1, waiting for transfers between devices, local(): lax.all_gather(w_in, 'dp', axis=0, tiled=True)  321 us
    reduce_scatter x1, waiting for transfers between devices, local(): lax.psum_scatter(gradients[0].astype(jnp.bfloat16), 'dp', scatter_dimensi...  289 us
    dot_general x16, matrix products, span_step(): within = jnp.einsum('hij,jhp->ihp', weights, driven, precision=PRECISE)  145 us
    all_gather x1, waiting for transfers between devices, local(): lax.all_gather(w_out, 'dp', axis=0, tiled=True)  140 us
    unnamed x2, blocking collectives  69.2 us
    all_to_all x1, waiting for transfers between devices, local(): lax.all_to_all(head_part.astype(jnp.bfloat16), 'seq', split_axis=1, conca...  66.8 us
    dot_general x20, matrix products, span_step(): jnp.einsum('in,hpn->ihp', c_block, memory, precision=PRECISE)  52.8 us
    another operation x98, local copies, waits for them, and re-layouts  51.8 us
  transfers between devices with their start and end apart: 14, of which 6 were waited for; matrix products, arithmetic and copies ran while one was open for 42% of the time, Pallas kernels for 0%

commit v1 on v0

v1 whole, which is shorter than its diff:
```python
import functools

import jax
import jax.numpy as jnp
from jax import lax
from jax.experimental import pallas as pl
from jax.experimental.pallas import tpu as pltpu
from jax.sharding import PartitionSpec as P

Q = 128
EXACT = lax.Precision.HIGHEST
EPSILON = 1e-05
LOG2E = 1.4426950408889634
RESET = 160.0
F32 = jnp.float32
BF16 = jnp.bfloat16


def sigmoid(x):
    return 0.5 * jnp.tanh(0.5 * x) + 0.5


def softplus(x):
    return jnp.maximum(x, 0.0) + jnp.log1p(jnp.exp(-jnp.abs(x)))


def nt(a, b):
    return lax.dot_general(a, b, (((1,), (1,)), ((), ())), preferred_element_type=F32)


def mm(a, b):
    return jnp.dot(a, b, preferred_element_type=F32)


def decays(pj, cols, hp, width):
    arg = pj[0, :, width + 256 : width + 384].astype(F32) + hp[0:1, :]
    dt = softplus(arg)
    rows = lax.broadcasted_iota(jnp.int32, (Q, Q), 0)
    lanes = lax.broadcasted_iota(jnp.int32, (Q, Q), 1)
    lower = (rows >= lanes).astype(F32)
    level = jnp.dot(lower, dt * hp[1:2, :], precision=EXACT, preferred_element_type=F32)
    level = level + cols[0, :, 3:4]
    return arg, dt, level, rows, lanes


def fwd_kernel(pairs, pj, cols, sg, hp, ch, pre, ys, gn, st, red, state, tail):
    width = pairs * 256
    inner = pairs * 128
    chunk = pl.program_id(1)

    @pl.when(chunk == 0)
    def _():
        state[...] = jnp.zeros_like(state)
        tail[...] = jnp.zeros_like(tail)

    _, dt, level, rows, lanes = decays(pj, cols, hp, width)
    level_t = level.T
    low = lanes < 64
    masks = [cols[0, :, d : d + 1] for d in range(3)]

    def conv(raw, at):
        ext = jnp.concatenate([tail[:, at : at + 128], raw], axis=0)
        total = raw * ch[3:4, at : at + 128] + ch[4:5, at : at + 128]
        for d in (1, 2, 3):
            moved = pltpu.roll(ext, d, 0)[8:]
            total = total + moved * masks[d - 1] * ch[3 - d : 4 - d, at : at + 128]
        tail[:, at : at + 128] = raw[Q - 8 :]
        pre[0, :, at : at + 128] = total
        return total * sigmoid(total)

    b_rows = conv(pj[0, :, width : width + 128].astype(F32), inner)
    c_rows = conv(pj[0, :, width + 128 : width + 256].astype(F32), inner + 128)
    b_t = b_rows.T.astype(BF16)
    b_low = b_rows.astype(BF16)
    c_low = c_rows.astype(BF16)
    scores = jnp.where(rows >= lanes, nt(c_low, b_low), 0.0)
    old = state[...].astype(BF16)
    st[0, 0] = old
    carried_all = mm(c_low, old)
    squares = jnp.zeros((Q, 128), F32)
    cross = jnp.zeros((Q, 128), F32)
    for p in range(pairs):
        at = p * 128
        one = pj[0, :, p * 256 : p * 256 + 128].astype(F32)
        two = pj[0, :, p * 256 + 128 : p * 256 + 256].astype(F32)
        z = jnp.where(low, one, pltpu.roll(two, 64, 1))
        v = jnp.where(low, pltpu.roll(one, 64, 1), two)
        xc = conv(v, at)
        l0 = jnp.broadcast_to(level[:, 2 * p : 2 * p + 1], (Q, Q))
        l1 = jnp.broadcast_to(level[:, 2 * p + 1 : 2 * p + 2], (Q, Q))
        le = jnp.where(low, l0, l1)
        dte = jnp.where(low, dt[:, 2 * p : 2 * p + 1], dt[:, 2 * p + 1 : 2 * p + 2])
        u = xc * dte
        w0 = jnp.exp2(jnp.minimum(l0 - level_t[2 * p : 2 * p + 1, :], 0.0)) * scores
        w1 = jnp.exp2(jnp.minimum(l1 - level_t[2 * p + 1 : 2 * p + 2, :], 0.0)) * scores
        wide = jnp.concatenate([w0.astype(BF16), w1.astype(BF16)], axis=1)
        blocks = jnp.concatenate(
            [jnp.where(low, u, 0.0).astype(BF16), jnp.where(low, 0.0, u).astype(BF16)], axis=0
        )
        part = mm(wide, blocks) + carried_all[:, at : at + 128] * jnp.exp2(le)
        ys[0, :, at : at + 128] = part
        gated = (part + ch[5:6, at : at + 128] * xc) * (z * sigmoid(z))
        scaled = gated * ch[6:7, at : at + 128]
        gn[0, :, at : at + 128] = scaled.astype(BF16)
        squares = squares + gated * gated
        cross = cross + sg[0, :, at : at + 128].astype(F32) * scaled
        last = le[Q - 1 : Q, :]
        ul = (u * jnp.exp2(last - le)).astype(BF16)
        state[:, at : at + 128] = state[:, at : at + 128] * jnp.exp2(last) + mm(b_t, ul)
    both = jnp.where(
        lanes == 0, jnp.sum(squares, axis=1, keepdims=True), jnp.sum(cross, axis=1, keepdims=True)
    )
    red[0] = both.T[0:8]


def mix_forward(pj, cols, sg, hp, ch, interpret=False):
    seqs, length, total = pj.shape
    width = total - 384
    inner = width // 2
    pairs = inner // 128
    chunks = length // Q

    def row(n):
        return pl.BlockSpec((1, Q, n), lambda s, c: (s, c, 0))

    def whole(a):
        return pl.BlockSpec(a.shape, lambda s, c: (0,) * a.ndim)

    return pl.pallas_call(
        functools.partial(fwd_kernel, pairs),
        grid=(seqs, chunks),
        in_specs=[row(total), row(128), row(inner), whole(hp), whole(ch)],
        out_specs=[
            row(inner + 256),
            row(inner),
            row(inner),
            pl.BlockSpec((1, 1, 128, inner), lambda s, c: (s, c, 0, 0)),
            pl.BlockSpec((1, 8, Q), lambda s, c: (s, 0, c)),
        ],
        out_shape=[
            jax.ShapeDtypeStruct((seqs, length, inner + 256), F32),
            jax.ShapeDtypeStruct((seqs, length, inner), F32),
            jax.ShapeDtypeStruct((seqs, length, inner), BF16),
            jax.ShapeDtypeStruct((seqs, chunks, 128, inner), BF16),
            jax.ShapeDtypeStruct((seqs, 8, length), F32),
        ],
        scratch_shapes=[pltpu.VMEM((128, inner), F32), pltpu.VMEM((8, inner + 256), F32)],
        compiler_params=pltpu.CompilerParams(vmem_limit_bytes=48 * 2**20),
        name="mix_forward",
    )(pj, cols, sg, hp, ch)


def bwd_kernel(
    pairs, pj, cols, cols2, sg, pre, ys, st, hp, ch, sel, pg, chacc, hacc,
    dstate, halo, edy_all, ul_all,
):
    width = pairs * 256
    inner = pairs * 128
    first = (pl.program_id(0) == 0) & (pl.program_id(1) == 0)

    @pl.when(pl.program_id(1) == 0)
    def _():
        dstate[...] = jnp.zeros_like(dstate)
        halo[...] = jnp.zeros_like(halo)

    @pl.when(first)
    def _():
        chacc[...] = jnp.zeros_like(chacc)
        hacc[...] = jnp.zeros_like(hacc)

    arg, dt, level, rows, lanes = decays(pj, cols, hp, width)
    level_t = level.T
    low = lanes < 64
    masks = [cols[0, :, 3 + d : 4 + d] for d in (1, 2, 3)]
    rho = jnp.broadcast_to(cols2[0, :, 0:1], (Q, 128))
    k2 = jnp.broadcast_to(cols2[0, :, 1:2], (Q, 128))

    def fold(x):
        return jnp.sum(x.reshape(Q // 8, 8, 128), axis=0)

    def conv_back(grad, raw, at):
        ext = jnp.concatenate([grad, halo[:, at : at + 128]], axis=0)
        out = grad * ch[3:4, at : at + 128]
        chacc[3, :, at : at + 128] += fold(grad * raw)
        chacc[4, :, at : at + 128] += fold(grad)
        for d in (1, 2, 3):
            moved = pltpu.roll(ext, Q + 8 - d, 0)[:Q] * masks[d - 1]
            out = out + moved * ch[3 - d : 4 - d, at : at + 128]
            chacc[3 - d, :, at : at + 128] += fold(moved * raw)
        halo[:, at : at + 128] = grad[:8]
        return out

    pre_b = pre[0, :, inner : inner + 128]
    pre_c = pre[0, :, inner + 128 : inner + 256]
    sig_b, sig_c = sigmoid(pre_b), sigmoid(pre_c)
    b_rows, c_rows = pre_b * sig_b, pre_c * sig_c
    b_low, c_low = b_rows.astype(BF16), c_rows.astype(BF16)
    c_t = c_rows.T.astype(BF16)
    upper = lanes >= rows
    scores = jnp.where(upper, nt(b_low, c_low), 0.0)
    dlow = dstate[...].astype(BF16)
    dsb_all = mm(b_low, dlow)
    dscores = jnp.zeros((Q, Q), F32)
    sums = jnp.zeros((6 * Q, 128), F32)
    keep = jnp.zeros((8, 128), F32)
    for p in range(pairs):
        at = p * 128
        one = pj[0, :, p * 256 : p * 256 + 128].astype(F32)
        two = pj[0, :, p * 256 + 128 : p * 256 + 256].astype(F32)
        z = jnp.where(low, one, pltpu.roll(two, 64, 1))
        v = jnp.where(low, pltpu.roll(one, 64, 1), two)
        pr = pre[0, :, at : at + 128]
        sp = sigmoid(pr)
        xc = pr * sp
        l0 = jnp.broadcast_to(level[:, 2 * p : 2 * p + 1], (Q, Q))
        l1 = jnp.broadcast_to(level[:, 2 * p + 1 : 2 * p + 2], (Q, Q))
        le = jnp.where(low, l0, l1)
        dte = jnp.where(low, dt[:, 2 * p : 2 * p + 1], dt[:, 2 * p + 1 : 2 * p + 2])
        u = xc * dte
        skip = ch[5:6, at : at + 128]
        part = ys[0, :, at : at + 128]
        y = part + skip * xc
        sz = sigmoid(z)
        silz = z * sz
        gated = y * silz
        graw = sg[0, :, at : at + 128].astype(F32)
        scaled_rho = graw * rho
        chacc[5, :, at : at + 128] += fold(scaled_rho * gated)
        gg = scaled_rho * ch[6:7, at : at + 128] - k2 * gated
        dy = gg * silz
        dz = gg * y * (sz + silz * (1.0 - sz))
        ulow = u.astype(BF16)
        dylow = dy.astype(BF16)
        w0 = jnp.exp2(jnp.minimum(level_t[2 * p : 2 * p + 1, :] - l0, 0.0))
        w1 = jnp.exp2(jnp.minimum(level_t[2 * p + 1 : 2 * p + 2, :] - l1, 0.0))
        wide = jnp.concatenate([(w0 * scores).astype(BF16), (w1 * scores).astype(BF16)], axis=1)
        dyb = jnp.concatenate(
            [jnp.where(low, dy, 0.0).astype(BF16), jnp.where(low, 0.0, dy).astype(BF16)], axis=0
        )
        ub = jnp.concatenate(
            [jnp.where(low, u, 0.0).astype(BF16), jnp.where(low, 0.0, u).astype(BF16)], axis=0
        )
        duw = mm(wide, dyb)
        gt = nt(ub, dylow)
        dscores = dscores + w0 * gt[:Q] + w1 * gt[Q:]
        last = le[Q - 1 : Q, :]
        lve = jnp.exp2(last - le)
        edy = (dy * jnp.exp2(le)).astype(BF16)
        ul = (u * lve).astype(BF16)
        edy_all[:, at : at + 128] = edy
        ul_all[:, at : at + 128] = ul
        dsb = dsb_all[:, at : at + 128]
        du = duw + lve * dsb
        r1 = dylow.astype(F32) * part - ulow.astype(F32) * duw
        r2 = ul.astype(F32) * dsb
        r1h, r2h = r1.astype(BF16), r2.astype(BF16)
        stacked = jnp.concatenate(
            [
                r1h,
                (r1 - r1h.astype(F32)).astype(BF16),
                r2h,
                (r2 - r2h.astype(F32)).astype(BF16),
                (dy * xc).astype(BF16),
                (du * xc).astype(BF16),
            ],
            axis=0,
        )
        sums = sums + mm(stacked, sel[p])
        decay = jnp.exp2(last)
        kept = fold(dlow[:, at : at + 128].astype(F32) * st[0, 0, :, at : at + 128].astype(F32)) * decay
        kept_high = kept.astype(BF16)
        keep = keep + mm(kept_high, sel[p]) + mm((kept - kept_high.astype(F32)).astype(BF16), sel[p])
        dstate[:, at : at + 128] = dstate[:, at : at + 128] * decay + mm(c_t, edy)
        dv = conv_back((du * dte + skip * dy) * (sp + xc * (1.0 - sp)), v, at)
        pg[0, :, p * 256 : p * 256 + 128] = jnp.where(low, dz, pltpu.roll(dv, 64, 1)).astype(BF16)
        pg[0, :, p * 256 + 128 : p * 256 + 256] = jnp.where(low, pltpu.roll(dz, 64, 1), dv).astype(BF16)
    dsc = jnp.where(upper, dscores, 0.0)
    db = mm(dsc.astype(BF16), c_low) + nt(ul_all[...], dlow)
    dc = mm(dsc.T.astype(BF16), b_low) + nt(edy_all[...], st[0, 0])
    raw_b = pj[0, :, width : width + 128].astype(F32)
    raw_c = pj[0, :, width + 128 : width + 256].astype(F32)
    pg[0, :, width : width + 128] = conv_back(
        db * (sig_b + b_rows * (1.0 - sig_b)), raw_b, inner
    ).astype(BF16)
    pg[0, :, width + 128 : width + 256] = conv_back(
        dc * (sig_c + c_rows * (1.0 - sig_c)), raw_c, inner + 128
    ).astype(BF16)
    r1 = sums[:Q] + sums[Q : 2 * Q]
    r2 = sums[2 * Q : 3 * Q] + sums[3 * Q : 4 * Q]
    da = (
        jnp.dot(upper.astype(F32), r1, precision=EXACT, preferred_element_type=F32)
        + jnp.dot((rows > lanes).astype(F32), r2, precision=EXACT, preferred_element_type=F32)
        + jnp.sum(keep, axis=0, keepdims=True)
    )
    ddt = da * hp[2:3, :] + sums[5 * Q :]
    ds = ddt * sigmoid(arg)
    pg[0, :, width + 256 : width + 384] = ds.astype(BF16)
    hacc[0] += fold(ds)
    hacc[1] += fold(da * dt)
    hacc[2] += fold(sums[4 * Q : 5 * Q])


def mix_backward(pj, cols, cols2, sg, pre, ys, st, hp, ch, sel):
    seqs, length, total = pj.shape
    width = total - 384
    inner = width // 2
    pairs = inner // 128
    chunks = length // Q

    def row(n):
        return pl.BlockSpec((1, Q, n), lambda s, c: (s, chunks - 1 - c, 0))

    def whole(shape):
        return pl.BlockSpec(shape, lambda s, c: (0,) * len(shape))

    return pl.pallas_call(
        functools.partial(bwd_kernel, pairs),
        grid=(seqs, chunks),
        in_specs=[
            row(total),
            row(128),
            row(128),
            row(inner),
            row(inner + 256),
            row(inner),
            pl.BlockSpec((1, 1, 128, inner), lambda s, c: (s, chunks - 1 - c, 0, 0)),
            whole(hp.shape),
            whole(ch.shape),
            whole(sel.shape),
        ],
        out_specs=[row(total), whole((6, 8, inner + 256)), whole((3, 8, 128))],
        out_shape=[
            jax.ShapeDtypeStruct((seqs, length, total), BF16),
            jax.ShapeDtypeStruct((6, 8, inner + 256), F32),
            jax.ShapeDtypeStruct((3, 8, 128), F32),
        ],
        scratch_shapes=[
            pltpu.VMEM((128, inner), F32),
            pltpu.VMEM((8, inner + 256), F32),
            pltpu.VMEM((Q, inner), BF16),
            pltpu.VMEM((Q, inner), BF16),
        ],
        compiler_params=pltpu.CompilerParams(vmem_limit_bytes=48 * 2**20),
        name="mix_backward",
    )(pj, cols, cols2, sg, pre, ys, st, hp, ch, sel)


def columns(seg):
    seqs, length = seg.shape
    back = [
        jnp.pad((seg[:, d:] == seg[:, :-d]).astype(F32), ((0, 0), (d, 0))) for d in (1, 2, 3)
    ]
    ahead = [
        jnp.pad((seg[:, d:] == seg[:, :-d]).astype(F32), ((0, 0), (0, d))) for d in (1, 2, 3)
    ]
    ends = seg.reshape(seqs, length // Q, Q)[:, :, -1]
    before = jnp.pad(ends[:, :-1], ((0, 0), (1, 0)))
    level = -RESET * (seg.reshape(seqs, length // Q, Q) - before[:, :, None]).astype(F32)
    stacked = jnp.stack([*back, level.reshape(seqs, length), *ahead], axis=-1)
    return jnp.pad(stacked, ((0, 0), (0, 0), (0, 121)))


def selectors(pairs):
    lane = lax.broadcasted_iota(jnp.int32, (pairs, 128, 128), 1)
    pair = lax.broadcasted_iota(jnp.int32, (pairs, 128, 128), 0)
    out = lax.broadcasted_iota(jnp.int32, (pairs, 128, 128), 2)
    return (out == 2 * pair + lane // 64).astype(BF16)


def local(
    tokens,
    segment_ids,
    w_in,
    w_out,
    conv_weight,
    conv_bias,
    norm_gain,
    gated_gain,
    dt_bias,
    a_log,
    skip_weight,
    cotangent,
):
    groups = lax.axis_size("seq")
    shards = lax.axis_size("dp")
    place = lax.axis_index("seq")
    owner = lax.axis_index("dp")
    seqs, part, model = tokens.shape
    length = part * groups
    rows_out = w_out.shape[0]
    wide = rows_out * shards
    heads = dt_bias.shape[0]
    size = wide // heads
    mine = heads // groups
    inner = mine * size
    span = 2 * inner
    taps = conv_weight.shape[1]
    state2 = w_in.shape[1] - 2 * wide - heads
    channels = wide + state2
    share = channels // shards
    small = jnp.concatenate(
        [conv_weight.reshape(-1), conv_bias, norm_gain, gated_gain]
    ).astype(F32)
    small = lax.all_gather(small, "dp", axis=0, tiled=False)
    cuts = [share * taps, share * (taps + 1), share * (taps + 1) + norm_gain.shape[0]]
    conv_w = small[:, : cuts[0]].reshape(channels, taps)
    conv_b = small[:, cuts[0] : cuts[1]].reshape(channels)
    norm_all = small[:, cuts[1] : cuts[2]].reshape(-1)
    gain_all = small[:, cuts[2] :].reshape(-1)

    def own(a):
        return lax.dynamic_slice_in_dim(a, place * inner, inner, 0)

    def own_heads(a):
        return lax.dynamic_slice_in_dim(a, place * mine, mine, 0)

    floats = tokens.astype(F32)
    inverse = lax.rsqrt(jnp.mean(floats * floats, axis=-1, keepdims=True) + EPSILON)
    unit = floats * inverse
    normed = lax.all_gather((unit * norm_all).astype(BF16), "seq", axis=1, tiled=True)
    cot = lax.all_gather(cotangent, "seq", axis=1, tiled=True)
    w_mine = jnp.concatenate(
        [
            lax.dynamic_slice_in_dim(w_in, place * span, span, 1),
            w_in[:, 2 * wide : 2 * wide + state2],
            jnp.pad(
                lax.dynamic_slice_in_dim(w_in, 2 * wide + state2 + place * mine, mine, 1),
                ((0, 0), (0, 128 - mine)),
            ),
        ],
        axis=1,
    )
    w_full = lax.all_gather(w_mine, "dp", axis=0, tiled=True)
    ratio = shards // groups
    held = jnp.where(
        (owner // ratio == place) & (jnp.arange(ratio)[:, None, None] == owner % ratio),
        w_out[None],
        jnp.zeros((), BF16),
    ).reshape(inner, model)
    wo = lax.psum(held, "dp")
    sg = jnp.einsum("std,cd->stc", cot, wo, preferred_element_type=F32).astype(BF16)
    pj = jnp.einsum("std,de->ste", normed, w_full, preferred_element_type=F32).astype(BF16)

    def pad(v):
        return jnp.pad(v, (0, 128 - mine))

    rate = -jnp.exp(own_heads(a_log))
    hp = jnp.stack([pad(own_heads(dt_bias)), pad(rate * LOG2E), pad(rate)] + [jnp.zeros(128)] * 5)
    blank = jnp.zeros((state2,), F32)
    ch = jnp.concatenate(
        [
            jnp.concatenate([own(conv_w), conv_w[wide:]]).T,
            jnp.concatenate([own(conv_b), conv_b[wide:]])[None],
            jnp.concatenate([jnp.repeat(own_heads(skip_weight), size), blank])[None],
            jnp.concatenate([own(gain_all), blank])[None],
            jnp.zeros((1, inner + state2), F32),
        ]
    )
    cols = columns(segment_ids)
    pre, ys, gn, st, red = mix_forward(pj, cols, sg, hp, ch)
    totals = lax.psum(red[:, :2], "seq")
    rho = lax.rsqrt(totals[:, 0] / wide + EPSILON)
    k2 = rho**3 * totals[:, 1] / wide
    cols2 = jnp.pad(jnp.stack([rho, k2], axis=-1), ((0, 0), (0, 0), (0, 126)))
    product = jnp.einsum("stc,cd->std", gn, wo, preferred_element_type=F32)
    product = (product * rho[:, :, None]).astype(BF16)
    result = (
        floats
        + lax.psum_scatter(product, "seq", scatter_dimension=1, tiled=True).astype(F32)
    ).astype(BF16)
    cot_rho = (cot.astype(F32) * rho[:, :, None]).astype(BF16)
    wo_grad = jnp.einsum("stc,std->cd", gn, cot_rho, preferred_element_type=F32).astype(BF16)
    wo_grad = lax.psum(wo_grad, "dp").reshape(ratio, rows_out, model)
    wo_grad = lax.dynamic_index_in_dim(wo_grad, owner % ratio, 0, False)
    wo_grad = lax.psum(jnp.where(owner // ratio == place, wo_grad, jnp.zeros((), BF16)), "seq")
    pg, chacc, hacc = mix_backward(
        pj, cols, cols2, sg, pre, ys, st, hp, ch, selectors(inner // 128)
    )
    win_grad = jnp.einsum("std,ste->de", normed, pg, preferred_element_type=F32).astype(BF16)
    win_grad = lax.psum_scatter(win_grad, "dp", scatter_dimension=0, tiled=True)
    win_grad = lax.all_gather(win_grad, "seq", axis=0, tiled=False).astype(F32)
    rows_in = win_grad.shape[1]
    w_in_grad = jnp.concatenate(
        [
            win_grad[:, :, :span].transpose(1, 0, 2).reshape(rows_in, 2 * wide),
            jnp.sum(win_grad[:, :, span : span + state2], axis=0),
            win_grad[:, :, span + state2 : span + state2 + mine]
            .transpose(1, 0, 2)
            .reshape(rows_in, heads),
        ],
        axis=1,
    )
    ngrad = jnp.einsum("ste,de->std", pg, w_full, preferred_element_type=F32).astype(BF16)
    ngrad = lax.psum_scatter(ngrad, "seq", scatter_dimension=1, tiled=True).astype(F32)
    unit_grad = ngrad * norm_all
    tokens_grad = cotangent.astype(F32) + inverse * (
        unit_grad - unit * jnp.mean(unit_grad * unit, axis=-1, keepdims=True)
    )
    chsum = jnp.sum(chacc, axis=1)
    hsum = jnp.sum(hacc, axis=1)[:, :mine]
    hsum = hsum * jnp.stack([jnp.ones((mine,)), rate, jnp.ones((mine,))])

    def spread(a, n, start):
        full = jnp.zeros(a.shape[:-1] + (n,), F32)
        return lax.dynamic_update_slice_in_dim(full, a, start, a.ndim - 1)

    chan = jnp.concatenate(
        [spread(chsum[:, :inner], wide, place * inner), chsum[:, inner:]], axis=1
    )
    packed = jnp.concatenate(
        [
            chan[: taps + 1].reshape(-1),
            chan[taps + 1, :wide],
            jnp.sum(ngrad * unit, axis=(0, 1)),
            spread(hsum, heads, place * mine).reshape(-1),
        ]
    )
    packed = lax.psum(packed, ("dp", "seq"))
    chan = packed[: (taps + 1) * channels].reshape(taps + 1, channels)
    chan = lax.dynamic_slice_in_dim(chan, owner * share, share, 1)
    at = (taps + 1) * channels
    gain_grad = lax.dynamic_slice_in_dim(packed[at : at + wide], owner * rows_out, rows_out, 0)
    at += wide
    norm_grad = lax.dynamic_slice_in_dim(packed[at : at + model], owner * rows_in, rows_in, 0)
    at += model
    return (
        result,
        tokens_grad,
        w_in_grad,
        wo_grad.astype(F32),
        chan[:taps].T,
        chan[taps],
        norm_grad,
        gain_grad,
        packed[at : at + heads],
        packed[at + heads : at + 2 * heads],
        packed[at + 2 * heads : at + 3 * heads],
    )


def solution(mesh):
    return jax.shard_map(
        local,
        mesh=mesh,
        in_specs=(
            P("dp", "seq", None),
            P("dp", None),
            P("dp", None),
            P("dp", None),
            P("dp", None),
            P("dp"),
            P("dp"),
            P("dp"),
            P(),
            P(),
            P(),
            P("dp", "seq", None),
        ),
        out_specs=(
            P("dp", "seq", None),
            P("dp", "seq", None),
            P("dp", None),
            P("dp", None),
            P("dp", None),
            P("dp"),
            P("dp"),
            P("dp"),
            P(),
            P(),
            P(),
        ),
        check_vma=False,
    )
```

time: 2360 us -> 789 us (0.33)
  local copies, waits for them, and re-layouts: 579 us -> 30.5 us
  waiting for transfers between devices: 843 us -> 523 us
  other arithmetic: 324 us -> 27.9 us
  matrix products: 355 us -> 82.1 us
  blocking collectives: 183 us -> 35.9 us
  Pallas kernels: 0 us -> 70.1 us
  starting transfers between devices: 29 us -> 0.69 us
    all_gather x3 -> x4, waiting for transfers between devices: 474 us -> 95.8 us  [the longest x1 72.9 us: local(): w_full = lax.all_gather(w_mine, 'dp', axis=0, tiled=True)]
    dot_general x78 -> x6, matrix products: 355 us -> 82.1 us  [the longest x1 18.9 us: local(): jnp.einsum('std,ste->de', normed, pg, preferred_element_type=F32)]
    psum x1 -> x4, waiting for transfers between devices: 12.1 us -> 251 us  [the longest x1 122 us: local(): packed = lax.psum(packed, ('dp', 'seq'))]
    reduce_scatter x3, waiting for transfers between devices: 289 us -> 176 us  [the longest x1 113 us: local(): win_grad = lax.psum_scatter(win_grad, 'dp', scatter_dimension=0, tiled=True)]
    reshape x33 -> x10, local copies, waits for them, and re-layouts: 116 us -> 6.08 us  [the longest x1 2.94 us: local(): conv_w = small[:, :cuts[0]].reshape(channels, taps)]
    reduce_sum x18 -> x4, other arithmetic: 90 us -> 2.73 us  [the longest x1 2.62 us: local(): jnp.sum(ngrad * unit, axis=(0, 1))]
    convert_element_type x12 -> x0, local copies, waits for them, and re-layouts: 73.9 us -> none  [the longest x1 36.7 us: local(): head_part.astype(jnp.bfloat16)]
    mul x51 -> x3, other arithmetic: 70.6 us -> 0.1 us  [the longest x1 0.08 us: local(): rate * LOG2E]
  transfers between devices with their start and end apart: 14 -> 11, of which waited for: 6 -> 9; matrix products, arithmetic and copies ran while one was open for 42% -> 12% of each run, Pallas kernels for 0% -> 6%
where the time goes in v1:
time: 789 us; the launch traced here: 786 us
  waiting for transfers between devices  523 us (66%)
  matrix products  82.1 us (10%)
  Pallas kernels  70.1 us (9%)
  blocking collectives  35.9 us (5%)
  local copies, waits for them, and re-layouts  30.5 us (4%)
  other arithmetic  27.9 us (4%)
  between operations  16.3 us (2%)
    psum x1, waiting for transfers between devices, local(): packed = lax.psum(packed, ('dp', 'seq'))  122 us
    reduce_scatter x1, waiting for transfers between devices, local(): win_grad = lax.psum_scatter(win_grad, 'dp', scatter_dimension=0, tiled=True)  113 us
    all_gather x1, waiting for transfers between devices, local(): w_full = lax.all_gather(w_mine, 'dp', axis=0, tiled=True)  72.9 us
    psum x1, waiting for transfers between devices, local(): wo = lax.psum(held, 'dp')  69 us
    reduce_scatter x1, waiting for transfers between devices, local(): lax.psum_scatter(product, 'seq', scatter_dimension=1, tiled=True)  57.6 us
    pallas_call x1, Pallas kernels, mix_backward(): pl.pallas_call(functools.partial(bwd_kernel, pairs), grid=(seqs, chunks),...  45.1 us
    psum x1, waiting for transfers between devices, local(): lax.psum(jnp.where(owner // ratio == place, wo_grad, jnp.zeros((), BF16))...  39.7 us
    all_gather x1, blocking collectives, local(): small = lax.all_gather(small, 'dp', axis=0, tiled=False)  25.9 us
  transfers between devices with their start and end apart: 11, of which 9 were waited for; matrix products, arithmetic and copies ran while one was open for 12% of the time, Pallas kernels for 6%

profile of v1, /device:TPU:3, one launch (start us, length us, event | category | flops | bytes accessed | tf_op | source)
XLA Modules:
  0.0 786.4 jit_solution(4443018775029310753)
XLA Ops:
  8.2 3.0 bitcast_select_fusion
  12.5 25.9 %all-gather.1 = f32[8,1,2656]{2,1,0:T(1,128)S(1)} all-gather(f32[1,1,2656]{2,1,0:T(1,128)S(1)} %bitcast_convert_fusion.2), channel_id=1, replica_groups=mesh['dp'=8,'seq'=4] {'dp'}, dimensions={0}, use_global_device_ids=true | all-gather | bytes 95616 | tf_op jit(solution)/shard_map/all_gather | solution.py:404
  39.0 1.6 fusion.19
  48.1 2.9 reshape.200
  53.6 69.0 %all-reduce.20.cloned.1.call-done = bf16[768,1536]{1,0:T(8,128)(2,1)} async-done(((bf16[768,1536]{1,0:T(8,128)(2,1)}), bf16[768,1536]{1,0:T(8,128)(2,1)}) %all-reduce.20.cloned.1.call-update) | async-done | bytes 2359312 | tf_op jit(solution)/shard_map/psum | solution.py:440
  122.7 9.0 %convert_bitcast_fusion.sg = bf16[2,1024,768]{2,1,0:T(8,128)(2,1)} fusion(bf16[2,1024,1536]{2,1,0:T(8,128)(2,1)} %all-gather.11.cloned.1.call-done, bf16[768,1536]{1,0:T(8,128)(2,1)} %all-reduce.20.cloned.1.call-done), kind=kOutput, calls=%fused_computation.30 | convolution fusion | flops 4833411072 | bytes 11796480 | tf_op jit(solution)/shard_map/std,cd->stc/dot_general | solution.py:441
  131.7 72.9 %all-gather.9.cloned.1.call-done = bf16[1536,1920]{1,0:T(8,128)(2,1)} async-done(((bf16[192,1920]{1,0:T(8,128)(2,1)}), bf16[1536,1920]{1,0:T(8,128)(2,1)}) %all-gather.9.cloned.1.call-update) | async-done | bytes 5898256 | tf_op jit(solution)/shard_map/all_gather | solution.py:433
  204.6 18.4 %fusion.6.pj = bf16[2,1024,1920]{2,1,0:T(8,128)(2,1)} fusion(bf16[2,1024,1536]{2,1,0:T(8,128)(2,1)} %all-gather.7.cloned.1.call-done, bf16[1536,1920]{1,0:T(8,128)(2,1)} %all-gather.9.cloned.1.call-done), kind=kOutput, calls=%fused_computation.9 | convolution fusion | flops 12083527680 | bytes 20054016 | tf_op jit(solution)/shard_map/std,de->ste/dot_general | solution.py:442
  223.0 25.0 %mix_forward.1 = (f32[2,1024,1024]{2,1,0:T(8,128)}, f32[2,1024,768]{2,1,0:T(8,128)}, bf16[2,1024,768]{2,1,0:T(8,128)(2,1)S(1)}, bf16[2,8,128,768]{3,2,1,0:T(8,128)(2,1)}, f32[2,8,1024]{2,1,0:T(8,128)S(1)}) custom-call(bf16[2,1024,1920]{2,1,0:T(8,128)(2,1)} %fusion.6.pj, f32[2,1024,128]{2,1,0:T(8,128)S(1)} %pad.60.cols, ...), custom_call_target="tpu_custom_call" | custom-call | tf_op jit(solution)/shard_map/mix_forward/pallas_call | solution.py:129
  248.1 1.6 copy-done.1
  249.7 10.0 %psum.36 = f32[2,2,1024]{2,1,0:T(2,128)S(1)} all-reduce(f32[2,2,1024]{2,1,0:T(2,128)S(1)} %slice.123), channel_id=1, replica_groups=mesh['dp'=8,'seq'=4] {'seq'}, use_global_device_ids=true, to_apply=%region_2.3 | all-reduce | flops 4096 | bytes 32768 | tf_op jit(solution)/shard_map/psum | solution.py:461
  259.7 9.8 %bitcast_convert_fusion.1 = bf16[768,1536]{1,0:T(8,128)(2,1)} fusion(bf16[2,1024,768]{2,1,0:T(8,128)(2,1)} %copy-done.1, bf16[2,1024,1536]{2,1,0:T(8,128)(2,1)} %all-gather.11.cloned.1.call-done, f32[2,1024]{1,0:T(2,128)S(1)} %bitcast.117), kind=kOutput, calls=%fused_computation.20 | convolution fusion | flops 4842455040 | bytes 11804672 | tf_op jit(solution)/shard_map/stc,std->cd/dot_general | solution.py:472
  272.3 2.0 fusion.30
  275.2 45.1 %mix_backward.1 = (bf16[2,1024,1920]{2,1,0:T(8,128)(2,1)}, f32[6,8,1024]{2,1,0:T(8,128)S(1)}, f32[3,8,128]{2,1,0:T(8,128)S(1)}) custom-call(bf16[2,1024,1920]{2,1,0:T(8,128)(2,1)} %fusion.6.pj, f32[2,1024,128]{2,1,0:T(8,128)S(1)} %pad.60.cols, f32[2,1024,128]{2,1,0:T(8,128)S(1)} %select_maximum_fusion.cols2, bf16[2,1024,768]{2,1,0:T(8,128)(2,1)S(1)} %copy-done, ...), custom_call_target="tpu_custom_call" | custom-call | tf_op jit(solution)/shard_map/mix_backward/pallas_call | solution.py:316
  320.2 16.9 %fusion.9 = bf16[2,1024,1536]{2,1,0:T(8,128)(2,1)} fusion(bf16[2,1024,1920]{2,1,0:T(8,128)(2,1)} %get-tuple-element.24, bf16[1536,1920]{1,0:T(8,128)(2,1)S(1)} %bitcast.128), kind=kOutput, calls=%fused_computation.10 | convolution fusion | flops 12082741248 | bytes 20054016 | tf_op jit(solution)/shard_map/ste,de->std/dot_general | solution.py:493
  337.4 18.9 %bitcast_convert_fusion = bf16[1536,1920]{1,0:T(8,128)(2,1)} fusion(bf16[2,1024,1536]{2,1,0:T(8,128)(2,1)} %all-gather.7.cloned.1.call-done, bf16[2,1024,1920]{2,1,0:T(8,128)(2,1)} %get-tuple-element.24), kind=kOutput, calls=%fused_computation.2 | convolution fusion | flops 12082544640 | bytes 20054016 | tf_op jit(solution)/shard_map/std,ste->de/dot_general | solution.py:479
  356.4 20.5 %all-reduce.22.cloned.1.call-done = bf16[2,384,1536]{2,1,0:T(8,128)(2,1)} async-done(((bf16[2,384,1536]{2,1,0:T(8,128)(2,1)}), bf16[2,384,1536]{2,1,0:T(8,128)(2,1)}) %all-reduce.22.cloned.1.call-update) | async-done | bytes 2359312 | tf_op jit(solution)/shard_map/psum | solution.py:473
  376.9 2.4 select_bitcast_fusion
  379.4 9.1 %multiply_convert_fusion.1 = bf16[2,1024,1536]{2,1,0:T(8,128)(2,1)} fusion(bf16[2,1024,768]{2,1,0:T(8,128)(2,1)} %copy-done.1, f32[2,1024]{1,0:T(2,128)S(1)} %bitcast.119, bf16[768,1536]{1,0:T(8,128)(2,1)} %all-reduce.20.cloned.1.call-done), kind=kOutput, calls=%fused_computation.1 | convolution fusion | flops 4838129664 | bytes 11804672 | tf_op jit(solution)/shard_map/stc,cd->std/dot_general | solution.py:465
  389.1 5.4 reduce-scatter.6.cloned.1.call-done
  394.5 2.6 fusion.21
  397.9 112.7 %reduce-scatter.8.cloned.1.call-done = bf16[192,1920]{1,0:T(8,128)(2,1)} async-done(((bf16[1536,1920]{1,0:T(8,128)(2,1)}), bf16[192,1920]{1,0:T(8,128)(2,1)}) %reduce-scatter.8.cloned.1.call-update) | async-done | bytes 737296 | tf_op jit(solution)/shard_map/reduce_scatter | solution.py:480
  510.5 39.7 %all-reduce.24.cloned.1.call-done = bf16[384,1536]{1,0:T(8,128)(2,1)} async-done(((bf16[384,1536]{1,0:T(8,128)(2,1)}), bf16[384,1536]{1,0:T(8,128)(2,1)}) %all-reduce.24.cloned.1.call-update) | async-done | bytes 1179664 | tf_op jit(solution)/shard_map/psum | solution.py:475
  550.2 3.0 convert_element_type.124
  553.2 57.6 %reduce-scatter.4.cloned.1.call-done = bf16[2,256,1536]{2,1,0:T(8,128)(2,1)} async-done(((bf16[2,1024,1536]{2,1,0:T(8,128)(2,1)}), bf16[2,256,1536]{2,1,0:T(8,128)(2,1)}) %reduce-scatter.4.cloned.1.call-update) | async-done | bytes 1572880 | tf_op jit(solution)/shard_map/reduce_scatter | solution.py:469
  610.7 5.4 fusion.18
  616.1 121.7 %all-reduce.26.cloned.1.call-done = f32[21392]{0:T(1024)} async-done(((f32[21392]{0:T(1024)}), f32[21392]{0:T(1024)}) %all-reduce.26.cloned.1.call-update) | async-done | bytes 85584 | tf_op jit(solution)/shard_map/psum | solution.py:518
  744.1 22.9 %all-gather.13.cloned.1.call-done = bf16[768,1920]{1,0:T(8,128)(2,1)} async-done(((bf16[192,1920]{1,0:T(8,128)(2,1)}), bf16[768,1920]{1,0:T(8,128)(2,1)}) %all-gather.13.cloned.1.call-update) | async-done | bytes 2949136 | tf_op jit(solution)/shard_map/all_gather | solution.py:481
  768.0 2.2 convert
  770.2 2.8 slice_bitcast_fusion
  773.4 2.8 copy.128
  776.2 2.6 pad_maximum_fusion
  (159 shorter events, 24.7 us)
Async XLA Ops:
  8.0 114.7 %all-reduce.20.cloned.1.call-start = ((), (), s32[]{:S(2)}) async-start(), calls=%async_computation.5 | async-start | bytes 4718592 | tf_op jit(solution)/shard_map/psum | solution.py:440
  8.2 3.7 copy-start.10
  8.2 3.8 copy-start.8
  8.2 3.8 copy-start.7
  8.2 3.8 copy-start.6
  8.2 30.4 %copy-start.2 = (bf16[2,256,1536]{2,1,0:T(8,128)(2,1)S(1)}, bf16[2,256,1536]{2,1,0:T(8,128)(2,1)}, u32[]{:S(2)}) copy-start(bf16[2,256,1536]{2,1,0:T(8,128)(2,1)} %param.12) | copy-start | bytes 4718596
  11.3 111.4 %all-gather.11.cloned.1.call-start = ((), (), s32[]{:S(2)}) async-start(), calls=%async_computation.6 | async-start | bytes 7864320 | tf_op jit(solution)/shard_map/all_gather | solution.py:421
  11.9 119.8 %all-gather.7.cloned.1.call-start = ((), (), s32[]{:S(2)}) async-start(), calls=%async_computation.3 | async-start | bytes 7864320 | tf_op jit(solution)/shard_map/all_gather | solution.py:420
  39.0 4.0 slice-start
  40.6 3.5 copy-start.11
  40.6 3.5 copy-start.12
  40.6 3.8 copy-start.5
  40.6 164.0 %all-gather.9.cloned.1.call-start = ((), (), s32[]{:S(2)}) async-start(), calls=%async_computation.4 | async-start | bytes 6635520 | tf_op jit(solution)/shard_map/all_gather | solution.py:433
  43.9 333.0 %all-reduce.22.cloned.1.call-start = ((), (), s32[]{:S(2)}) async-start(), calls=%async_computation.10 | async-start | bytes 4718592 | tf_op jit(solution)/shard_map/psum | solution.py:473
  45.5 7.8 copy-start.9
  248.1 1.6 copy-start.1
  269.6 124.9 %reduce-scatter.6.cloned.1.call-start = ((), (), s32[]{:S(2)}) async-start(), calls=%async_computation.8 | async-start | bytes 7864320 | tf_op jit(solution)/shard_map/reduce_scatter | solution.py:494
  272.3 2.0 copy-start.3
  272.3 2.8 copy-start
  274.4 45.9 %slice-start.1 = ((s8[5898240]{0:T(1024)(128)(4,1)}), s8[1703936]{0:T(1024)(128)(4,1)S(1)}, s32[]{:S(2)}) async-start(s8[5898240]{0:T(1024)(128)(4,1)} %bitcast.127), calls=%async_computation.15 | async-start | bytes 3407872
  275.2 45.1 %slice-start.2 = ((s8[5898240]{0:T(1024)(128)(4,1)}), s8[4194304]{0:T(1024)(128)(4,1)S(1)}, s32[]{:S(2)}) async-start(s8[5898240]{0:T(1024)(128)(4,1)} %bitcast.127), calls=%async_computation.16 | async-start | bytes 8388608
  337.2 173.4 %reduce-scatter.8.cloned.1.call-start = ((), (), s32[]{:S(2)}) async-start(), calls=%async_computation.9 | async-start | bytes 6635520 | tf_op jit(solution)/shard_map/reduce_scatter | solution.py:480
  356.3 193.9 %all-reduce.24.cloned.1.call-start = ((), (), s32[]{:S(2)}) async-start(), calls=%async_computation.11 | async-start | bytes 2359296 | tf_op jit(solution)/shard_map/psum | solution.py:475
  379.4 231.4 %reduce-scatter.4.cloned.1.call-start = ((), (), s32[]{:S(2)}) async-start(), calls=%async_computation.7 | async-start | bytes 7864320 | tf_op jit(solution)/shard_map/reduce_scatter | solution.py:469
  388.5 349.3 %all-reduce.26.cloned.1.call-start = ((), (), s32[]{:S(2)}) async-start(), calls=%async_computation.12 | async-start | bytes 172032 | tf_op jit(solution)/shard_map/psum | solution.py:518
  389.1 221.6 %copy-start.4 = (bf16[2,256,1536]{2,1,0:T(8,128)(2,1)S(1)}, bf16[2,256,1536]{2,1,0:T(8,128)(2,1)}, u32[]{:S(2)}) copy-start(bf16[2,256,1536]{2,1,0:T(8,128)(2,1)} %param.23) | copy-start | bytes 4718596
  397.8 369.2 %all-gather.13.cloned.1.call-start = ((), (), s32[]{:S(2)}) async-start(), calls=%async_computation.13 | async-start | bytes 3686400 | tf_op jit(solution)/shard_map/all_gather | solution.py:481
Sparse Core Ops, SparseCore 0:
  13.0 109.6 all-reduce.19
  269.7 107.1 all-reduce.21
Sparse Core Ops, SparseCore 1:
  13.3 46.7 all-gather.10
  62.1 46.2 all-gather.6
  111.0 93.5 all-gather.8
  337.2 57.2 reduce-scatter.5
  398.2 112.3 reduce-scatter.7
  513.6 36.5 all-reduce.23
  552.8 57.9 reduce-scatter.3
  616.8 121.0 all-reduce.25
  739.3 27.7 all-gather.12

commit v2 on v1

--- a/solution.py
+++ b/solution.py
@@ -14,6 +14,9 @@
 RESET = 160.0
 F32 = jnp.float32
 BF16 = jnp.bfloat16
+LUMPS = 6
+WOFF = 1
+MESH = pl.DeviceIdType.MESH
 
 
 def sigmoid(x):
@@ -367,6 +370,365 @@
     return (out == 2 * pair + lane // 64).astype(BF16)
 
 
+def gather_kernel(
+    dims, wm, wo_in, small_in, tok_in, cot_in,
+    normed_o, cot_o, pj_o, sg_o, w_o, wo_o, small_o,
+    tok, cot, wbig, wo, small, pjv, sgv,
+    szu, szd, rz, sy, ry, wsu, wsd, wrz, wsy, wry, bx_s, bx_r, bc_s, bc_r, loc, out,
+):
+    deep, pieces, rows, inner, part, length = dims
+    d = lax.axis_index("dp")
+    s = lax.axis_index("seq")
+    z = d // 2
+    y = d % 2
+    top = deep - 1
+    up, down, side = (d + 2, s), (d - 2, s), (d + 1 - 2 * y, s)
+    across, twin = (d, s + 2 - 4 * (s // 2)), (d, s + 1 - 2 * (s % 2))
+    opposite = across[1]
+
+    bar = pltpu.get_barrier_semaphore()
+
+    @pl.when(z < top)
+    def _():
+        pl.semaphore_signal(bar, inc=1, device_id=up, device_id_type=MESH)
+
+    @pl.when(z > 0)
+    def _():
+        pl.semaphore_signal(bar, inc=1, device_id=down, device_id_type=MESH)
+
+    for who in (side, across, twin):
+        pl.semaphore_signal(bar, inc=1, device_id=who, device_id_type=MESH)
+    pl.semaphore_wait(bar, 3 + jnp.minimum(z, 1) + jnp.minimum(top - z, 1))
+
+    def send(src, dst, ssem, rsem, who):
+        return pltpu.make_async_remote_copy(
+            src_ref=src, dst_ref=dst, send_sem=ssem, recv_sem=rsem,
+            device_id=who, device_id_type=MESH,
+        )
+
+    width = 2 * inner
+
+    def cols(k):
+        return pl.ds(width, 384) if k == 1 else pl.ds((k - 2) * 256, 256)
+
+    def held(k, owner):
+        if k == 0:
+            return small.at[owner]
+        return wbig.at[pl.ds(pl.multiple_of(owner * rows, 16), rows), cols(k)]
+
+    def source(k):
+        return small_in.at[...] if k == 0 else wm.at[:, cols(k)]
+
+    def own_send(k):
+        src, dst = source(k), held(k, d)
+
+        @pl.when(z < top)
+        def _():
+            send(src, dst, szu.at[k, z], rz.at[k, z], up).start()
+
+        @pl.when(z > 0)
+        def _():
+            send(src, dst, szd.at[k, z], rz.at[k, z], down).start()
+
+        send(src, dst, sy.at[k, z], ry.at[k, z], side).start()
+
+    def hop(k, h):
+        below, above = z - h, z + h
+
+        @pl.when(below >= 0)
+        def _():
+            ref = held(k, below * 2 + y)
+            send(ref, ref, szu.at[k, below], rz.at[k, below], up).wait_recv()
+
+            @pl.when(z < top)
+            def _():
+                send(ref, ref, szu.at[k, below], rz.at[k, below], up).start()
+
+            send(ref, ref, sy.at[k, below], ry.at[k, below], side).start()
+
+        @pl.when(above <= top)
+        def _():
+            ref = held(k, above * 2 + y)
+            send(ref, ref, szd.at[k, above], rz.at[k, above], down).wait_recv()
+
+            @pl.when(z > 0)
+            def _():
+                send(ref, ref, szd.at[k, above], rz.at[k, above], down).start()
+
+            send(ref, ref, sy.at[k, above], ry.at[k, above], side).start()
+
+    def arrive(k):
+        for e in range(deep):
+            ref = held(k, e * 2 + 1 - y)
+            send(ref, ref, sy.at[k, e], ry.at[k, e], side).wait_recv()
+
+    def own_copy(src, dst, sem):
+        return pltpu.make_async_copy(src, dst, sem)
+
+    here = pl.multiple_of(s * part, 16)
+    there = pl.multiple_of(opposite * part, 16)
+    locals_ = [
+        own_copy(small_in, small.at[d], loc.at[0]),
+        own_copy(wm, wbig.at[pl.ds(pl.multiple_of(d * rows, 16), rows)], loc.at[1]),
+    ]
+    for q in range(2):
+        locals_.append(own_copy(tok_in.at[q], tok.at[q, pl.ds(here, part)], loc.at[2 + q]))
+        locals_.append(own_copy(cot_in.at[q], cot.at[q, pl.ds(here, part)], loc.at[4 + q]))
+    half = wo_in.shape[0]
+    mine = z == s
+
+    def root_copy():
+        return own_copy(wo_in, wo.at[pl.ds(pl.multiple_of(y * half, 16), half)], loc.at[6])
+
+    def block_sends(which, src, dst, q):
+        spot = dst.at[q, pl.ds(here, part)]
+        i = which * 2 + q
+        send(src.at[q], spot, bx_s.at[i], bx_r.at[i], across).start()
+        send(src.at[q], spot, bc_s.at[0, i], bc_r.at[0, i], twin).start()
+
+    def block_forward(which, dst, q):
+        spot = dst.at[q, pl.ds(there, part)]
+        i = which * 2 + q
+        send(spot, spot, bx_s.at[i], bx_r.at[i], across).wait_recv()
+        send(spot, spot, bc_s.at[1, i], bc_r.at[1, i], twin).start()
+
+    def block_arrive(which, dst, q):
+        i = which * 2 + q
+        for n in range(2):
+            spot = dst.at[q, pl.ds(here, part)]
+            send(spot, spot, bc_s.at[n, i], bc_r.at[n, i], twin).wait_recv()
+
+    lump = half // LUMPS
+
+    def wo_piece(i, col):
+        m = col * LUMPS + i
+        return m, wo.at[pl.ds(pl.multiple_of(m * lump, 16), lump)]
+
+    def wo_send(i, src=None):
+        m, ref = wo_piece(i, y)
+        src = ref if src is None else src
+
+        @pl.when((z >= s) & (z < top))
+        def _():
+            send(src, ref, wsu.at[m], wrz.at[m], up).start()
+
+        @pl.when((z <= s) & (z > 0))
+        def _():
+            send(src, ref, wsd.at[m], wrz.at[m], down).start()
+
+        send(src, ref, wsy.at[m], wry.at[m], side).start()
+
+    def wo_root(i):
+        @pl.when(mine)
+        def _():
+            wo_send(i, wo_in.at[pl.ds(i * lump, lump)])
+
+    def wo_hop(i, h):
+        @pl.when((z - s == h) | (s - z == h))
+        def _():
+            m, ref = wo_piece(i, y)
+            send(ref, ref, wsu.at[m], wrz.at[m], up).wait_recv()
+            wo_send(i)
+
+    def wo_arrive(i):
+        m, ref = wo_piece(i, 1 - y)
+        send(ref, ref, wsy.at[m], wry.at[m], side).wait_recv()
+
+    tile = 256
+
+    def project(k):
+        c = cols(k)
+
+        def step(i, _):
+            q, r = i // (length // tile), i % (length // tile)
+            at = pl.multiple_of(r * tile, tile)
+            pjv[q, pl.ds(at, tile), c] = mm(tok[q, pl.ds(at, tile), :], wbig[:, c]).astype(BF16)
+            return 0
+
+        lax.fori_loop(0, 2 * length // tile, step, 0)
+        own_copy(pjv.at[:, :, c], pj_o.at[:, :, c], out.at[k]).start()
+
+    for c in locals_:
+        c.start()
+
+    @pl.when(mine)
+    def _():
+        root_copy().start()
+
+    for q in range(2):
+        block_sends(0, tok_in, tok, q)
+    ahead = 3
+    for k in range(ahead):
+        own_send(k)
+    done = []
+
+    def hops(t):
+        for h in range(1, deep):
+            if 0 <= t - h < pieces:
+                hop(t - h, h)
+        for h in range(1, deep):
+            if 0 <= t - h - WOFF < LUMPS:
+                wo_hop(t - h - WOFF, h)
+        if 0 <= t - WOFF < LUMPS:
+            wo_root(t - WOFF)
+        if ahead <= t + ahead - 1 < pieces:
+            own_send(t + ahead - 1)
+
+    steps = max(pieces, WOFF + LUMPS) + deep - 1
+    count = dict(next=1)
+
+    def ready(n):
+        for _ in range(n):
+            if count["next"] < pieces:
+                arrive(count["next"])
+                project(count["next"])
+                count["next"] += 1
+
+    share = tok.shape[2] // (2 * deep)
+
+    def norm_step(i, _):
+        q, r = i // (length // 64), i % (length // 64)
+        at = pl.multiple_of(r * 64, 64)
+        x = tok[q, pl.ds(at, 64), :].astype(F32)
+        inv = lax.rsqrt(jnp.mean(x * x, axis=1, keepdims=True) + EPSILON)
+        gains = jnp.concatenate([small[e, 0:1, :share] for e in range(2 * deep)], axis=1)
+        tok[q, pl.ds(at, 64), :] = (x * inv * gains.astype(F32)).astype(BF16)
+        return 0
+
+    for t in range(1, steps):
+        hops(t)
+        if t == 3:
+            block_forward(0, tok, 0)
+        if t == 6:
+            block_forward(0, tok, 1)
+            for q in range(2):
+                block_sends(1, cot_in, cot, q)
+        if t == 7:
+            for i in (0, 1, 2, 4):
+                locals_[i].wait()
+            block_arrive(0, tok, 0)
+            block_arrive(0, tok, 1)
+            for q in range(2):
+                spot = tok.at[q, pl.ds(there, part)]
+                send(spot, spot, bc_s.at[1, q], bc_r.at[1, q], twin).wait_send()
+            arrive(0)
+            own_copy(small, small_o, out.at[0]).start()
+            lax.fori_loop(0, 2 * length // 64, norm_step, 0)
+            own_copy(tok, normed_o, out.at[pieces]).start()
+        if t > 7:
+            ready(1)
+    for i in range(LUMPS):
+        wo_arrive(i)
+
+    @pl.when(mine)
+    def _():
+        root_copy().wait()
+
+    block_forward(1, cot, 0)
+    ready(pieces)
+    own_copy(wbig, w_o, out.at[pieces + 1]).start()
+    own_copy(wo, wo_o, out.at[pieces + 2]).start()
+    block_forward(1, cot, 1)
+    locals_[3].wait()
+    locals_[5].wait()
+    block_arrive(1, cot, 0)
+    block_arrive(1, cot, 1)
+    own_copy(cot, cot_o, out.at[pieces + 3]).start()
+
+    def grad_step(i, _):
+        q, r = i // (length // tile), i % (length // tile)
+        at = pl.multiple_of(r * tile, tile)
+        sgv[q, pl.ds(at, tile), :] = nt(cot[q, pl.ds(at, tile), :], wo[...]).astype(BF16)
+        return 0
+
+    lax.fori_loop(0, 2 * length // tile, grad_step, 0)
+    own_copy(sgv, sg_o, out.at[pieces + 4]).start()
+
+    for k in range(pieces):
+        for e in range(deep):
+            ref = held(k, e * 2 + y)
+
+            @pl.when((z >= e) & (z < top))
+            def _():
+                send(ref, ref, szu.at[k, e], rz.at[k, e], up).wait_send()
+
+            @pl.when((z <= e) & (z > 0))
+            def _():
+                send(ref, ref, szd.at[k, e], rz.at[k, e], down).wait_send()
+
+            send(ref, ref, sy.at[k, e], ry.at[k, e], side).wait_send()
+    for i in range(LUMPS):
+        m, ref = wo_piece(i, y)
+
+        @pl.when((z >= s) & (z < top))
+        def _():
+            send(ref, ref, wsu.at[m], wrz.at[m], up).wait_send()
+
+        @pl.when((z <= s) & (z > 0))
+        def _():
+            send(ref, ref, wsd.at[m], wrz.at[m], down).wait_send()
+
+        send(ref, ref, wsy.at[m], wry.at[m], side).wait_send()
+    for which, dst in ((0, tok), (1, cot)):
+        for q in range(2):
+            i = which * 2 + q
+            spot = dst.at[q, pl.ds(here, part)]
+            send(spot, spot, bx_s.at[i], bx_r.at[i], across).wait_send()
+            for n in range(1 + which):
+                send(spot, spot, bc_s.at[n, i], bc_r.at[n, i], twin).wait_send()
+    own_copy(small, small_o, out.at[0]).wait()
+    for k in range(1, pieces):
+        own_copy(pjv.at[:, :, cols(k)], pj_o.at[:, :, cols(k)], out.at[k]).wait()
+    own_copy(tok, normed_o, out.at[pieces]).wait()
+    own_copy(wbig, w_o, out.at[pieces + 1]).wait()
+    own_copy(wo, wo_o, out.at[pieces + 2]).wait()
+    own_copy(cot, cot_o, out.at[pieces + 3]).wait()
+    own_copy(sgv, sg_o, out.at[pieces + 4]).wait()
+
+
+def gather(wm, w_out, small, tokens, cotangent, shards, groups):
+    rows, total = wm.shape
+    width = total - 384
+    inner = width // 2
+    seqs, part, model = tokens.shape
+    length = part * groups
+    deep = shards // 2
+    pairs = inner // 128
+    pieces = pairs + 2
+    any_ = pl.BlockSpec(memory_space=pl.ANY)
+    dma = pltpu.SemaphoreType.DMA
+    small_rows, small_cols = small.shape
+    full = (shards * rows, total)
+    shapes = [
+        (seqs, length, model), (seqs, length, model), (seqs, length, total), (seqs, length, inner),
+        full, (inner, model), (shards, small_rows, small_cols),
+    ]
+    return pl.pallas_call(
+        functools.partial(gather_kernel, (deep, pieces, rows, inner, part, length)),
+        in_specs=[any_] * 5,
+        out_specs=[any_] * 7,
+        out_shape=[jax.ShapeDtypeStruct(n, BF16) for n in shapes],
+        scratch_shapes=[
+            pltpu.VMEM(shapes[0], BF16),
+            pltpu.VMEM(shapes[0], BF16),
+            pltpu.VMEM(full, BF16),
+            pltpu.VMEM((inner, model), BF16),
+            pltpu.VMEM(shapes[6], BF16),
+            pltpu.VMEM(shapes[2], BF16),
+            pltpu.VMEM(shapes[3], BF16),
+            dma((pieces, deep)), dma((pieces, deep)), dma((pieces, deep)),
+            dma((pieces, deep)), dma((pieces, deep)),
+            *[dma((2 * LUMPS,))] * 5,
+            dma((4,)), dma((4,)), dma((2, 4)), dma((2, 4)),
+            dma((7,)), dma((pieces + 5,)),
+        ],
+        compiler_params=pltpu.CompilerParams(
+            collective_id=1, has_side_effects=True, vmem_limit_bytes=56 * 2**20
+        ),
+        name="gather_project",
+    )(wm, w_out, small, tokens, cotangent)
+
+
 def local(
     tokens,
     segment_ids,
@@ -398,48 +760,68 @@
     state2 = w_in.shape[1] - 2 * wide - heads
     channels = wide + state2
     share = channels // shards
-    small = jnp.concatenate(
-        [conv_weight.reshape(-1), conv_bias, norm_gain, gated_gain]
-    ).astype(F32)
-    small = lax.all_gather(small, "dp", axis=0, tiled=False)
-    cuts = [share * taps, share * (taps + 1), share * (taps + 1) + norm_gain.shape[0]]
-    conv_w = small[:, : cuts[0]].reshape(channels, taps)
-    conv_b = small[:, cuts[0] : cuts[1]].reshape(channels)
-    norm_all = small[:, cuts[1] : cuts[2]].reshape(-1)
-    gain_all = small[:, cuts[2] :].reshape(-1)
-
-    def own(a):
-        return lax.dynamic_slice_in_dim(a, place * inner, inner, 0)
-
-    def own_heads(a):
-        return lax.dynamic_slice_in_dim(a, place * mine, mine, 0)
-
-    floats = tokens.astype(F32)
-    inverse = lax.rsqrt(jnp.mean(floats * floats, axis=-1, keepdims=True) + EPSILON)
-    unit = floats * inverse
-    normed = lax.all_gather((unit * norm_all).astype(BF16), "seq", axis=1, tiled=True)
-    cot = lax.all_gather(cotangent, "seq", axis=1, tiled=True)
+    ratio = shards // groups
+    step_cols = jnp.pad(
+        lax.dynamic_slice_in_dim(w_in, 2 * wide + state2 + place * mine, mine, 1),
+        ((0, 0), (0, 128 - mine)),
+    )
     w_mine = jnp.concatenate(
         [
             lax.dynamic_slice_in_dim(w_in, place * span, span, 1),
             w_in[:, 2 * wide : 2 * wide + state2],
-            jnp.pad(
-                lax.dynamic_slice_in_dim(w_in, 2 * wide + state2 + place * mine, mine, 1),
-                ((0, 0), (0, 128 - mine)),
-            ),
+            step_cols,
         ],
         axis=1,
     )
-    w_full = lax.all_gather(w_mine, "dp", axis=0, tiled=True)
-    ratio = shards // groups
-    held = jnp.where(
-        (owner // ratio == place) & (jnp.arange(ratio)[:, None, None] == owner % ratio),
-        w_out[None],
-        jnp.zeros((), BF16),
-    ).reshape(inner, model)
-    wo = lax.psum(held, "dp")
-    sg = jnp.einsum("std,cd->stc", cot, wo, preferred_element_type=F32).astype(BF16)
-    pj = jnp.einsum("std,de->ste", normed, w_full, preferred_element_type=F32).astype(BF16)
+
+    def rows256(a):
+        flat = a.reshape(-1)
+        count = -(-flat.shape[0] // 256)
+        return jnp.pad(flat, (0, count * 256 - flat.shape[0])).reshape(count, 256), count
+
+    packs = [rows256(a) for a in (norm_gain, conv_bias, gated_gain, conv_weight)]
+    small = jnp.concatenate([p[0] for p in packs])
+    tall = -(-small.shape[0] // 16) * 16
+    small = jnp.pad(small, ((0, tall - small.shape[0]), (0, 0)))
+    floats = tokens.astype(F32)
+    inverse = lax.rsqrt(jnp.mean(floats * floats, axis=-1, keepdims=True) + EPSILON)
+    unit = floats * inverse
+    if shards == 8 and groups == 4:
+        normed, cot, pj, sg, w_full, wo, small_all = gather(
+            w_mine, w_out, small, tokens, cotangent, shards, groups
+        )
+    else:
+        small_all = lax.all_gather(small, "dp", axis=0, tiled=False)
+    small_all = small_all.astype(F32)
+    cut = [0]
+    for pack in packs:
+        cut.append(cut[-1] + pack[1])
+
+    def unpack(i, count):
+        return small_all[:, cut[i] : cut[i + 1]].reshape(shards, -1)[:, :count].reshape(-1)
+
+    norm_all = unpack(0, norm_gain.shape[0])
+    conv_b = unpack(1, share)
+    gain_all = unpack(2, rows_out)
+    conv_w = unpack(3, share * taps).reshape(channels, taps)
+    if not (shards == 8 and groups == 4):
+        normed = lax.all_gather((unit * norm_all).astype(BF16), "seq", axis=1, tiled=True)
+        cot = lax.all_gather(cotangent, "seq", axis=1, tiled=True)
+        w_full = lax.all_gather(w_mine, "dp", axis=0, tiled=True)
+        held = jnp.where(
+            (owner // ratio == place) & (jnp.arange(ratio)[:, None, None] == owner % ratio),
+            w_out[None],
+            jnp.zeros((), BF16),
+        ).reshape(inner, model)
+        wo = lax.psum(held, "dp")
+        sg = jnp.einsum("std,cd->stc", cot, wo, preferred_element_type=F32).astype(BF16)
+        pj = jnp.einsum("std,de->ste", normed, w_full, preferred_element_type=F32).astype(BF16)
+
+    def own(a):
+        return lax.dynamic_slice_in_dim(a, place * inner, inner, 0)
+
+    def own_heads(a):
+        return lax.dynamic_slice_in_dim(a, place * mine, mine, 0)
 
     def pad(v):
         return jnp.pad(v, (0, 128 - mine))

time: 789 us -> 705 us (0.89)
  waiting for transfers between devices: 523 us -> 385 us
  Pallas kernels: 70.1 us -> 183 us
  matrix products: 82.1 us -> 54.3 us
  blocking collectives: 35.9 us -> 9.44 us
    pallas_call x0 -> x1, Pallas kernels: none -> 113 us  [gather(): pl.pallas_call(functools.partial(gather_kernel, (deep, pieces, rows, inne...]
    all_gather x3 -> x0, waiting for transfers between devices: 72.9 us -> none  [the longest x1 72.9 us: local(): w_full = lax.all_gather(w_mine, 'dp', axis=0, tiled=True)]
    psum x1 -> x0, waiting for transfers between devices: 69 us -> none  [local(): wo = lax.psum(held, 'dp')]
    dot_general x2 -> x0, matrix products: 27.5 us -> none  [the longest x1 18.4 us: local(): jnp.einsum('std,de->ste', normed, w_full, preferred_element_type=F32)]
    all_gather x1 -> x0, blocking collectives: 25.9 us -> none  [local(): small = lax.all_gather(small, 'dp', axis=0, tiled=False)]
  transfers between devices with their start and end apart: 11 -> 7, of which waited for: 9 -> 7; matrix products, arithmetic and copies ran while one was open for 12% -> 10% of each run, Pallas kernels for 6% -> 6%
where the time goes in v2:
time: 705 us; the launch traced here: 702 us
  waiting for transfers between devices  385 us (55%)
  Pallas kernels  183 us (26%)
  matrix products  54.3 us (8%)
  local copies, waits for them, and re-layouts  28 us (4%)
  other arithmetic  25.4 us (4%)
  between operations  16.1 us (2%)
  blocking collectives  9.44 us (1%)
    psum x1, waiting for transfers between devices, local(): packed = lax.psum(packed, ('dp', 'seq'))  123 us
    pallas_call x1, Pallas kernels, gather(): pl.pallas_call(functools.partial(gather_kernel, (deep, pieces, rows, inne...  113 us
    reduce_scatter x1, waiting for transfers between devices, local(): win_grad = lax.psum_scatter(win_grad, 'dp', scatter_dimension=0, tiled=True)  113 us
    reduce_scatter x1, waiting for transfers between devices, local(): lax.psum_scatter(product, 'seq', scatter_dimension=1, tiled=True)  57.6 us
    pallas_call x1, Pallas kernels, mix_backward(): pl.pallas_call(functools.partial(bwd_kernel, pairs), grid=(seqs, chunks),...  45 us
    psum x1, waiting for transfers between devices, local(): lax.psum(jnp.where(owner // ratio == place, wo_grad, jnp.zeros((), BF16))...  39.4 us
    psum x1, waiting for transfers between devices, local(): wo_grad = lax.psum(wo_grad, 'dp').reshape(ratio, rows_out, model)  28.3 us
    pallas_call x1, Pallas kernels, mix_forward(): pl.pallas_call(functools.partial(fwd_kernel, pairs), grid=(seqs, chunks),...  25.1 us
  transfers between devices with their start and end apart: 7, of which 7 were waited for; matrix products, arithmetic and copies ran while one was open for 10% of the time, Pallas kernels for 6%

profile of v2, /device:TPU:3, one launch (start us, length us, event | category | flops | bytes accessed | tf_op | source)
XLA Modules:
  0.0 702.2 jit_solution(5761381825824009867)
XLA Ops:
  12.7 0.9 slice.120
  15.5 1.3 constant_dynamic-slice_fusion.2
  16.9 0.9 fusion.20.wm
  18.4 113.0 %gather_project.1 = (bf16[2,1024,1536]{2,1,0:T(8,128)(2,1)}, bf16[2,1024,1536]{2,1,0:T(8,128)(2,1)}, bf16[2,1024,1920]{2,1,0:T(8,128)(2,1)}, bf16[2,1024,768]{2,...) custom-call(bf16[192,1920]{1,0:T(8,128)(2,1)} %fusion.20.wm, ...), custom_call_target="tpu_custom_call" | custom-call | tf_op jit(solution)/shard_map/gather_project/pallas_call | solution.py:706
  132.5 1.7 reshape_reshape.3
  136.3 25.1 %mix_forward.1 = (f32[2,1024,1024]{2,1,0:T(8,128)}, f32[2,1024,768]{2,1,0:T(8,128)}, bf16[2,1024,768]{2,1,0:T(8,128)(2,1)S(1)}, bf16[2,8,128,768]{3,2,1,0:T(8,128)(2,1)}, f32[2,8,1024]{2,1,0:T(8,128)S(1)}) custom-call(bf16[2,1024,1920]{2,1,0:T(8,128)(2,1)} %get-tuple-element.26.pj, f32[2,1024,128]{2,1,0:T(8,128)S(1)} %pad.85.cols, ...), custom_call_target="tpu_custom_call" | custom-call | tf_op jit(solution)/shard_map/mix_forward/pallas_call | solution.py:132
  161.4 1.7 copy-done.1
  163.1 9.4 %psum.28 = f32[2,2,1024]{2,1,0:T(2,128)S(1)} all-reduce(f32[2,2,1024]{2,1,0:T(2,128)S(1)} %slice.137), channel_id=1, replica_groups=mesh['dp'=8,'seq'=4] {'seq'}, use_global_device_ids=true, to_apply=%region_0.1 | all-reduce | flops 4096 | bytes 32768 | tf_op jit(solution)/shard_map/psum | solution.py:843
  172.6 9.8 %bitcast_convert_fusion.1 = bf16[768,1536]{1,0:T(8,128)(2,1)} fusion(bf16[2,1024,768]{2,1,0:T(8,128)(2,1)} %copy-done.1, bf16[2,1024,1536]{2,1,0:T(8,128)(2,1)} %get-tuple-element.38, f32[2,1024]{1,0:T(2,128)S(1)} %bitcast.110), kind=kOutput, calls=%fused_computation.13 | convolution fusion | flops 4842455040 | bytes 11804672 | tf_op jit(solution)/shard_map/stc,std->cd/dot_general | solution.py:854
  184.3 1.0 copy-done
  185.4 45.0 %mix_backward.1 = (bf16[2,1024,1920]{2,1,0:T(8,128)(2,1)}, f32[6,8,1024]{2,1,0:T(8,128)S(1)}, f32[3,8,128]{2,1,0:T(8,128)S(1)}) custom-call(bf16[2,1024,1920]{2,1,0:T(8,128)(2,1)} %get-tuple-element.26.pj, f32[2,1024,128]{2,1,0:T(8,128)S(1)} %pad.85.cols, f32[2,1024,128]{2,1,0:T(8,128)S(1)} %select_maximum_fusion.cols2, bf16[2,1024,768]{2,1,0:T(8,128)(2,1)S(1)} %copy-done, ...), custom_call_target="tpu_custom_call" | custom-call | tf_op jit(solution)/shard_map/mix_backward/pallas_call | solution.py:319
  230.4 16.9 %fusion.4 = bf16[2,1024,1536]{2,1,0:T(8,128)(2,1)} fusion(bf16[2,1024,1920]{2,1,0:T(8,128)(2,1)} %get-tuple-element.35, bf16[1536,1920]{1,0:T(8,128)(2,1)S(1)} %bitcast.122), kind=kOutput, calls=%fused_computation.7 | convolution fusion | flops 12082741248 | bytes 20054016 | tf_op jit(solution)/shard_map/ste,de->std/dot_general | solution.py:875
  247.3 19.1 %bitcast_convert_fusion = bf16[1536,1920]{1,0:T(8,128)(2,1)} fusion(bf16[2,1024,1536]{2,1,0:T(8,128)(2,1)} %get-tuple-element.37, bf16[2,1024,1920]{2,1,0:T(8,128)(2,1)} %get-tuple-element.35), kind=kOutput, calls=%fused_computation.2 | convolution fusion | flops 12082544640 | bytes 20054016 | tf_op jit(solution)/shard_map/std,ste->de/dot_general | solution.py:861
  266.5 28.3 %all-reduce.24.cloned.1.call-done = bf16[2,384,1536]{2,1,0:T(8,128)(2,1)} async-done(((bf16[2,384,1536]{2,1,0:T(8,128)(2,1)}), bf16[2,384,1536]{2,1,0:T(8,128)(2,1)}) %all-reduce.24.cloned.1.call-update) | async-done | bytes 2359312 | tf_op jit(solution)/shard_map/psum | solution.py:855
  294.8 2.4 select_bitcast_fusion
  297.4 8.5 %multiply_convert_fusion.1 = bf16[2,1024,1536]{2,1,0:T(8,128)(2,1)} fusion(bf16[2,1024,768]{2,1,0:T(8,128)(2,1)S(1)} %copy-done.2, f32[2,1024]{1,0:T(2,128)S(1)} %bitcast.112, bf16[768,1536]{1,0:T(8,128)(2,1)} %get-tuple-element.30), kind=kOutput, calls=%fused_computation.1 | convolution fusion | flops 4838129664 | bytes 11804672 | tf_op jit(solution)/shard_map/stc,cd->std/dot_general | solution.py:847
  308.0 1.2 reduce-scatter.6.cloned.1.call-done
  309.2 2.6 fusion.14
  312.5 112.9 %reduce-scatter.8.cloned.1.call-done = bf16[192,1920]{1,0:T(8,128)(2,1)} async-done(((bf16[1536,1920]{1,0:T(8,128)(2,1)}), bf16[192,1920]{1,0:T(8,128)(2,1)}) %reduce-scatter.8.cloned.1.call-update) | async-done | bytes 737296 | tf_op jit(solution)/shard_map/reduce_scatter | solution.py:862
  425.5 39.4 %all-reduce.26.cloned.1.call-done = bf16[384,1536]{1,0:T(8,128)(2,1)} async-done(((bf16[384,1536]{1,0:T(8,128)(2,1)}), bf16[384,1536]{1,0:T(8,128)(2,1)}) %all-reduce.26.cloned.1.call-update) | async-done | bytes 1179664 | tf_op jit(solution)/shard_map/psum | solution.py:857
  464.9 3.0 convert_element_type.112
  467.8 57.6 %reduce-scatter.4.cloned.1.call-done = bf16[2,256,1536]{2,1,0:T(8,128)(2,1)} async-done(((bf16[2,1024,1536]{2,1,0:T(8,128)(2,1)}), bf16[2,256,1536]{2,1,0:T(8,128)(2,1)}) %reduce-scatter.4.cloned.1.call-update) | async-done | bytes 1572880 | tf_op jit(solution)/shard_map/reduce_scatter | solution.py:851
  525.4 5.4 fusion.12
  530.8 122.7 %all-reduce.28.cloned.1.call-done = f32[21392]{0:T(1024)} async-done(((f32[21392]{0:T(1024)}), f32[21392]{0:T(1024)}) %all-reduce.28.cloned.1.call-update) | async-done | bytes 85584 | tf_op jit(solution)/shard_map/psum | solution.py:900
  653.6 0.9 slice.177
  658.5 1.4 fusion.35
  659.9 23.1 %all-gather.3.cloned.1.call-done = bf16[768,1920]{1,0:T(8,128)(2,1)} async-done(((bf16[192,1920]{1,0:T(8,128)(2,1)}), bf16[768,1920]{1,0:T(8,128)(2,1)}) %all-gather.3.cloned.1.call-update) | async-done | bytes 2949136 | tf_op jit(solution)/shard_map/all_gather | solution.py:863
  683.0 1.0 slice.173
  683.9 2.2 convert
  686.2 2.8 slice_bitcast_fusion
  689.4 2.8 copy.121
  692.1 2.6 pad_maximum_fusion
  (140 shorter events, 19.5 us)
Async XLA Ops:
  8.0 286.8 %all-reduce.24.cloned.1.call-start = ((), (), s32[]{:S(2)}) async-start(), calls=%async_computation.6 | async-start | bytes 4718592 | tf_op jit(solution)/shard_map/psum | solution.py:855
  18.4 115.9 %copy-start.7 = (f32[48]{0:T(128)S(1)}, f32[48]{0:T(128)}, u32[]{:S(2)}) copy-start(f32[48]{0:T(128)} %param.20) | copy-start | bytes 580
  18.4 116.0 %copy-start.8 = (f32[48]{0:T(128)S(1)}, f32[48]{0:T(128)}, u32[]{:S(2)}) copy-start(f32[48]{0:T(128)} %param.22) | copy-start | bytes 580
  18.4 116.1 %copy-start.6 = (f32[48]{0:T(128)S(1)}, f32[48]{0:T(128)}, u32[]{:S(2)}) copy-start(f32[48]{0:T(128)} %param.21) | copy-start | bytes 580
  18.4 116.3 %copy-start.5 = (s32[2,1024]{1,0:T(2,128)S(1)}, s32[2,1024]{1,0:T(2,128)}, u32[]{:S(2)}) copy-start(s32[2,1024]{1,0:T(2,128)} %param.13) | copy-start | bytes 24580
  161.4 1.7 copy-start.1
  182.4 126.7 %reduce-scatter.6.cloned.1.call-start = ((), (), s32[]{:S(2)}) async-start(), calls=%async_computation.4 | async-start | bytes 7864320 | tf_op jit(solution)/shard_map/reduce_scatter | solution.py:876
  183.5 1.9 copy-start
  183.8 46.5 %slice-start = ((s8[5898240]{0:T(1024)(128)(4,1)}), s8[1703936]{0:T(1024)(128)(4,1)S(1)}, s32[]{:S(2)}) async-start(s8[5898240]{0:T(1024)(128)(4,1)} %bitcast.121), calls=%async_computation.10 | async-start | bytes 3407872
  185.4 45.0 %slice-start.1 = ((s8[5898240]{0:T(1024)(128)(4,1)}), s8[4194304]{0:T(1024)(128)(4,1)S(1)}, s32[]{:S(2)}) async-start(s8[5898240]{0:T(1024)(128)(4,1)} %bitcast.121), calls=%async_computation.11 | async-start | bytes 8388608
  247.3 178.2 %reduce-scatter.8.cloned.1.call-start = ((), (), s32[]{:S(2)}) async-start(), calls=%async_computation.5 | async-start | bytes 6635520 | tf_op jit(solution)/shard_map/reduce_scatter | solution.py:862
  266.4 31.0 %copy-start.2 = (bf16[2,1024,768]{2,1,0:T(8,128)(2,1)S(1)}, bf16[2,1024,768]{2,1,0:T(8,128)(2,1)}, u32[]{:S(2)}) copy-start(bf16[2,1024,768]{2,1,0:T(8,128)(2,1)} %copy-done.1) | copy-start | bytes 9437188
  266.4 198.4 %all-reduce.26.cloned.1.call-start = ((), (), s32[]{:S(2)}) async-start(), calls=%async_computation.7 | async-start | bytes 2359296 | tf_op jit(solution)/shard_map/psum | solution.py:857
  297.2 228.2 %reduce-scatter.4.cloned.1.call-start = ((), (), s32[]{:S(2)}) async-start(), calls=%async_computation.3 | async-start | bytes 7864320 | tf_op jit(solution)/shard_map/reduce_scatter | solution.py:851
  306.0 1.6 copy-start.3
  306.0 347.6 %all-reduce.28.cloned.1.call-start = ((), (), s32[]{:S(2)}) async-start(), calls=%async_computation.8 | async-start | bytes 172032 | tf_op jit(solution)/shard_map/psum | solution.py:900
  307.9 217.5 %copy-start.4 = (bf16[2,256,1536]{2,1,0:T(8,128)(2,1)S(1)}, bf16[2,256,1536]{2,1,0:T(8,128)(2,1)}, u32[]{:S(2)}) copy-start(bf16[2,256,1536]{2,1,0:T(8,128)(2,1)} %cot_in.1) | copy-start | bytes 4718596
  312.5 370.5 %all-gather.3.cloned.1.call-start = ((), (), s32[]{:S(2)}) async-start(), calls=%async_computation.9 | async-start | bytes 3686400 | tf_op jit(solution)/shard_map/all_gather | solution.py:863
Sparse Core Ops, SparseCore 0:
  182.6 112.1 all-reduce.23
Sparse Core Ops, SparseCore 1:
  247.3 61.8 reduce-scatter.5
  313.1 112.2 reduce-scatter.7
  428.3 36.5 all-reduce.25
  467.4 57.9 reduce-scatter.3
  532.5 121.0 all-reduce.27
  655.2 27.7 all-gather.2

commit v3 on v2

--- a/solution.py
+++ b/solution.py
@@ -15,6 +15,7 @@
 F32 = jnp.float32
 BF16 = jnp.bfloat16
 LUMPS = 6
+PARTS = 5
 WOFF = 1
 MESH = pl.DeviceIdType.MESH
 
@@ -46,7 +47,7 @@
     return arg, dt, level, rows, lanes
 
 
-def fwd_kernel(pairs, pj, cols, sg, hp, ch, pre, ys, gn, st, red, state, tail):
+def fwd_kernel(pairs, pj, cols, sg, hp, ch, pre, ys, st, red, state, tail):
     width = pairs * 256
     inner = pairs * 128
     chunk = pl.program_id(1)
@@ -104,7 +105,6 @@
         ys[0, :, at : at + 128] = part
         gated = (part + ch[5:6, at : at + 128] * xc) * (z * sigmoid(z))
         scaled = gated * ch[6:7, at : at + 128]
-        gn[0, :, at : at + 128] = scaled.astype(BF16)
         squares = squares + gated * gated
         cross = cross + sg[0, :, at : at + 128].astype(F32) * scaled
         last = le[Q - 1 : Q, :]
@@ -136,14 +136,12 @@
         out_specs=[
             row(inner + 256),
             row(inner),
-            row(inner),
             pl.BlockSpec((1, 1, 128, inner), lambda s, c: (s, c, 0, 0)),
             pl.BlockSpec((1, 8, Q), lambda s, c: (s, 0, c)),
         ],
         out_shape=[
             jax.ShapeDtypeStruct((seqs, length, inner + 256), F32),
             jax.ShapeDtypeStruct((seqs, length, inner), F32),
-            jax.ShapeDtypeStruct((seqs, length, inner), BF16),
             jax.ShapeDtypeStruct((seqs, chunks, 128, inner), BF16),
             jax.ShapeDtypeStruct((seqs, 8, length), F32),
         ],
@@ -154,8 +152,8 @@
 
 
 def bwd_kernel(
-    pairs, pj, cols, cols2, sg, pre, ys, st, hp, ch, sel, pg, chacc, hacc,
-    dstate, halo, edy_all, ul_all,
+    pairs, pj, cols, rk, sg, pre, ys, st, hp, ch, sel, wo, wi, pg, chacc, hacc, sct, outp, ngp,
+    dstate, halo, edy_all, ul_all, sc_all,
 ):
     width = pairs * 256
     inner = pairs * 128
@@ -175,8 +173,9 @@
     level_t = level.T
     low = lanes < 64
     masks = [cols[0, :, 3 + d : 4 + d] for d in (1, 2, 3)]
-    rho = jnp.broadcast_to(cols2[0, :, 0:1], (Q, 128))
-    k2 = jnp.broadcast_to(cols2[0, :, 1:2], (Q, 128))
+    tall = jnp.concatenate([rk[0], jnp.zeros((Q - 8, Q), F32)], axis=0).T
+    rho = jnp.broadcast_to(tall[:, 0:1], (Q, 128))
+    k2 = jnp.broadcast_to(tall[:, 1:2], (Q, 128))
 
     def fold(x):
         return jnp.sum(x.reshape(Q // 8, 8, 128), axis=0)
@@ -228,7 +227,9 @@
         gated = y * silz
         graw = sg[0, :, at : at + 128].astype(F32)
         scaled_rho = graw * rho
-        chacc[5, :, at : at + 128] += fold(scaled_rho * gated)
+        scaled = gated * rho * ch[6:7, at : at + 128]
+        sct[at : at + 128, :] = scaled.T.astype(BF16)
+        sc_all[:, at : at + 128] = scaled.astype(BF16)
         gg = scaled_rho * ch[6:7, at : at + 128] - k2 * gated
         dy = gg * silz
         dz = gg * y * (sz + silz * (1.0 - sz))
@@ -301,14 +302,17 @@
     hacc[0] += fold(ds)
     hacc[1] += fold(da * dt)
     hacc[2] += fold(sums[4 * Q : 5 * Q])
-
-
-def mix_backward(pj, cols, cols2, sg, pre, ys, st, hp, ch, sel):
+    outp[0] = mm(sc_all[...], wo[...]).astype(BF16)
+    ngp[0] = nt(pg[0], wi[...]).astype(BF16)
+
+
+def mix_backward(pj, cols, rk, sg, pre, ys, st, hp, ch, sel, wo, wi):
     seqs, length, total = pj.shape
     width = total - 384
     inner = width // 2
     pairs = inner // 128
     chunks = length // Q
+    model = wo.shape[1]
 
     def row(n):
         return pl.BlockSpec((1, Q, n), lambda s, c: (s, chunks - 1 - c, 0))
@@ -322,7 +326,7 @@
         in_specs=[
             row(total),
             row(128),
-            row(128),
+            pl.BlockSpec((1, 8, Q), lambda s, c: (s, 0, chunks - 1 - c)),
             row(inner),
             row(inner + 256),
             row(inner),
@@ -330,22 +334,35 @@
             whole(hp.shape),
             whole(ch.shape),
             whole(sel.shape),
+            whole(wo.shape),
+            whole(wi.shape),
         ],
-        out_specs=[row(total), whole((6, 8, inner + 256)), whole((3, 8, 128))],
+        out_specs=[
+            row(total),
+            whole((5, 8, inner + 256)),
+            whole((3, 8, 128)),
+            pl.BlockSpec((inner, Q), lambda s, c: (0, s * chunks + chunks - 1 - c)),
+            row(model),
+            row(model),
+        ],
         out_shape=[
             jax.ShapeDtypeStruct((seqs, length, total), BF16),
-            jax.ShapeDtypeStruct((6, 8, inner + 256), F32),
+            jax.ShapeDtypeStruct((5, 8, inner + 256), F32),
             jax.ShapeDtypeStruct((3, 8, 128), F32),
+            jax.ShapeDtypeStruct((inner, seqs * length), BF16),
+            jax.ShapeDtypeStruct((seqs, length, model), BF16),
+            jax.ShapeDtypeStruct((seqs, length, model), BF16),
         ],
         scratch_shapes=[
             pltpu.VMEM((128, inner), F32),
             pltpu.VMEM((8, inner + 256), F32),
             pltpu.VMEM((Q, inner), BF16),
             pltpu.VMEM((Q, inner), BF16),
+            pltpu.VMEM((Q, inner), BF16),
         ],
         compiler_params=pltpu.CompilerParams(vmem_limit_bytes=48 * 2**20),
         name="mix_backward",
-    )(pj, cols, cols2, sg, pre, ys, st, hp, ch, sel)
+    )(pj, cols, rk, sg, pre, ys, st, hp, ch, sel, wo, wi)
 
 
 def columns(seg):
@@ -370,10 +387,54 @@
     return (out == 2 * pair + lane // 64).astype(BF16)
 
 
+def norm_kernel(wide, red, rk, got, ssem, rsem):
+    d = lax.axis_index("dp")
+    s = lax.axis_index("seq")
+    groups = got.shape[0]
+    bar = pltpu.get_barrier_semaphore()
+    for j in range(1, groups):
+        pl.semaphore_signal(bar, inc=1, device_id=(d, lax.rem(s + j, groups)), device_id_type=MESH)
+    pl.semaphore_wait(bar, groups - 1)
+    sends = [
+        pltpu.make_async_remote_copy(
+            src_ref=red, dst_ref=got.at[j], send_sem=ssem.at[j], recv_sem=rsem.at[j],
+            device_id=(d, lax.rem(s + j, groups)), device_id_type=MESH,
+        )
+        for j in range(1, groups)
+    ]
+    for copy in sends:
+        copy.start()
+    total = red[...]
+    for j, copy in enumerate(sends):
+        copy.wait()
+        total = total + got[j + 1]
+    rho = lax.rsqrt(total[:, 0:1] / wide + EPSILON)
+    rk[...] = jnp.concatenate(
+        [rho, rho * rho * rho * total[:, 1:2] / wide, jnp.zeros_like(total[:, 2:])], axis=1
+    )
+
+
+def norms(red, wide, groups):
+    vmem = pl.BlockSpec(memory_space=pltpu.VMEM)
+    return pl.pallas_call(
+        functools.partial(norm_kernel, wide),
+        in_specs=[vmem],
+        out_specs=vmem,
+        out_shape=jax.ShapeDtypeStruct(red.shape, F32),
+        scratch_shapes=[
+            pltpu.VMEM((groups, *red.shape), F32),
+            pltpu.SemaphoreType.DMA((groups,)),
+            pltpu.SemaphoreType.DMA((groups,)),
+        ],
+        compiler_params=pltpu.CompilerParams(collective_id=3, has_side_effects=True),
+        name="norms",
+    )(red)
+
+
 def gather_kernel(
     dims, wm, wo_in, small_in, tok_in, cot_in,
-    normed_o, cot_o, pj_o, sg_o, w_o, wo_o, small_o,
-    tok, cot, wbig, wo, small, pjv, sgv,
+    turned_o, cot_o, pj_o, sg_o, w_o, wo_o, small_o,
+    tok, cot, wbig, wo, small, pjv, sgv, turned,
     szu, szd, rz, sy, ry, wsu, wsd, wrz, wsy, wry, bx_s, bx_r, bc_s, bc_r, loc, out,
 ):
     deep, pieces, rows, inner, part, length = dims
@@ -614,7 +675,6 @@
             arrive(0)
             own_copy(small, small_o, out.at[0]).start()
             lax.fori_loop(0, 2 * length // 64, norm_step, 0)
-            own_copy(tok, normed_o, out.at[pieces]).start()
         if t > 7:
             ready(1)
     for i in range(LUMPS):
@@ -628,6 +688,17 @@
     ready(pieces)
     own_copy(wbig, w_o, out.at[pieces + 1]).start()
     own_copy(wo, wo_o, out.at[pieces + 2]).start()
+
+    def turn_step(i, _):
+        q, r = i // (length // tile), i % (length // tile)
+        at = pl.multiple_of(r * tile, tile)
+        to = pl.multiple_of(i * tile, tile)
+        for j in range(0, tok.shape[2], 128):
+            turned[j : j + 128, pl.ds(to, tile)] = tok[q, pl.ds(at, tile), j : j + 128].T
+        return 0
+
+    lax.fori_loop(0, 2 * length // tile, turn_step, 0)
+    own_copy(turned, turned_o, out.at[pieces]).start()
     block_forward(1, cot, 1)
     locals_[3].wait()
     locals_[5].wait()
@@ -679,7 +750,7 @@
     own_copy(small, small_o, out.at[0]).wait()
     for k in range(1, pieces):
         own_copy(pjv.at[:, :, cols(k)], pj_o.at[:, :, cols(k)], out.at[k]).wait()
-    own_copy(tok, normed_o, out.at[pieces]).wait()
+    own_copy(turned, turned_o, out.at[pieces]).wait()
     own_copy(wbig, w_o, out.at[pieces + 1]).wait()
     own_copy(wo, wo_o, out.at[pieces + 2]).wait()
     own_copy(cot, cot_o, out.at[pieces + 3]).wait()
@@ -700,7 +771,7 @@
     small_rows, small_cols = small.shape
     full = (shards * rows, total)
     shapes = [
-        (seqs, length, model), (seqs, length, model), (seqs, length, total), (seqs, length, inner),
+        (model, seqs * length), (seqs, length, model), (seqs, length, total), (seqs, length, inner),
         full, (inner, model), (shards, small_rows, small_cols),
     ]
     return pl.pallas_call(
@@ -709,13 +780,14 @@
         out_specs=[any_] * 7,
         out_shape=[jax.ShapeDtypeStruct(n, BF16) for n in shapes],
         scratch_shapes=[
-            pltpu.VMEM(shapes[0], BF16),
-            pltpu.VMEM(shapes[0], BF16),
+            pltpu.VMEM(shapes[1], BF16),
+            pltpu.VMEM(shapes[1], BF16),
             pltpu.VMEM(full, BF16),
             pltpu.VMEM((inner, model), BF16),
             pltpu.VMEM(shapes[6], BF16),
             pltpu.VMEM(shapes[2], BF16),
             pltpu.VMEM(shapes[3], BF16),
+            pltpu.VMEM(shapes[0], BF16),
             dma((pieces, deep)), dma((pieces, deep)), dma((pieces, deep)),
             dma((pieces, deep)), dma((pieces, deep)),
             *[dma((2 * LUMPS,))] * 5,
@@ -727,6 +799,406 @@
         ),
         name="gather_project",
     )(wm, w_out, small, tokens, cotangent)
+
+
+def greet(z, top, up, down, others):
+    bar = pltpu.get_barrier_semaphore()
+
+    @pl.when(z < top)
+    def _():
+        pl.semaphore_signal(bar, inc=1, device_id=up, device_id_type=MESH)
+
+    @pl.when(z > 0)
+    def _():
+        pl.semaphore_signal(bar, inc=1, device_id=down, device_id_type=MESH)
+
+    for who in others:
+        pl.semaphore_signal(bar, inc=1, device_id=who, device_id_type=MESH)
+    pl.semaphore_wait(bar, len(others) + jnp.minimum(z, 1) + jnp.minimum(top - z, 1))
+
+
+def send(src, dst, ssem, rsem, who):
+    return pltpu.make_async_remote_copy(
+        src_ref=src, dst_ref=dst, send_sem=ssem, recv_sem=rsem, device_id=who, device_id_type=MESH
+    )
+
+
+def add_into(dst, src):
+    count = dst.shape[0]
+    some = next(n for n in (64, 48, 32, 16) if count % n == 0)
+
+    def step(i, _):
+        at = pl.ds(pl.multiple_of(i * some, 16), some)
+        dst[at, :] = (dst[at, :].astype(F32) + src[at, :].astype(F32)).astype(BF16)
+        return 0
+
+    lax.fori_loop(0, count // some, step, 0)
+
+
+def scatter_kernel(
+    dims, nt_in, pg_in, st_in, cot_in, outp, ngp,
+    gw_o, wo_o, out_o, ng_o,
+    nt_v, pg_v, st_v, cot_v, pv, yb, zb, gath, tw, xr, stage, gw, ybw, zbw, wof,
+    sy, ry, su, sd, rz, gx_s, gx_r, gc_s, gc_r, tw_s, tw_r, xr_s, xr_r,
+    wy_s, wy_r, wu_s, wd_s, wz_r, bx_s, bx_r, bc_s, bc_r, loc, stg, out,
+):
+    deep, rows, part = dims
+    d = lax.axis_index("dp")
+    s = lax.axis_index("seq")
+    z = d // 2
+    y = d % 2
+    x = s // 2
+    c = s % 2
+    top = deep - 1
+    up, down, side = (d + 2, s), (d - 2, s), (d + 1 - 2 * y, s)
+    across, twin = (d, s + 2 - 4 * x), (d, s + 1 - 2 * c)
+    greet(z, top, up, down, (side, across, twin))
+    wide = pv.shape[1] // PARTS
+
+    def cut(k):
+        return pl.ds(k * wide, wide)
+
+    def lines(ref, i, count=rows):
+        return ref.at[pl.ds(pl.multiple_of(i * count, 16), count)]
+
+    loads = [
+        pltpu.make_async_copy(nt_in, nt_v, loc.at[0]),
+        *[
+            pltpu.make_async_copy(pg_in.at[:, cut(k)], pg_v.at[:, cut(k)], loc.at[3 + k])
+            for k in range(PARTS)
+        ],
+        pltpu.make_async_copy(st_in, st_v, loc.at[1]),
+        pltpu.make_async_copy(cot_in, cot_v, loc.at[2]),
+    ]
+    for load in loads:
+        load.start()
+
+    both = ((0, outp, out_o), (1, ngp, ng_o))
+
+    def token_rows(owner):
+        return pl.ds(pl.multiple_of(owner * part, 16), part)
+
+    def twin_send(n, ref, turn, q):
+        half = 1 - x if turn == 0 else x
+        return send(
+            ref.at[q, token_rows(2 * half + 1 - c)], tw.at[n, turn, q],
+            tw_s.at[n, turn, q], tw_r.at[n, turn, q], twin,
+        )
+
+    for n, ref, _ in both:
+        for turn in range(2):
+            for q in range(2):
+                twin_send(n, ref, turn, q).start()
+
+    def stage_copy(n, ref, turn, q):
+        half = 1 - x if turn == 0 else x
+        return pltpu.make_async_copy(ref.at[q, token_rows(2 * half + c)], stage.at[q], stg.at[q])
+
+    def pair_sum(n, ref, turn):
+        for q in range(2):
+            stage_copy(n, ref, turn, q).start()
+        for q in range(2):
+            twin_send(n, ref, turn, q).wait_recv()
+            stage_copy(n, ref, turn, q).wait()
+            add_into(tw.at[n, turn, q], stage.at[q])
+
+    def x_send(n, q):
+        return send(tw.at[n, 0, q], xr.at[n, q], xr_s.at[n, q], xr_r.at[n, q], across)
+
+    def x_start(n, ref):
+        pair_sum(n, ref, 0)
+        for q in range(2):
+            x_send(n, q).start()
+
+    def x_finish(n, dst):
+        for q in range(2):
+            x_send(n, q).wait_recv()
+            add_into(xr.at[n, q], tw.at[n, 1, q])
+            pltpu.make_async_copy(xr.at[n, q], dst.at[q], out.at[2 + 2 * n + q]).start()
+
+    def weigh(k):
+        def step(i, _):
+            at = pl.ds(pl.multiple_of(i * rows, 16), rows)
+            pv[at, cut(k)] = mm(nt_v[at, :], pg_v[:, cut(k)]).astype(BF16)
+            return 0
+
+        lax.fori_loop(0, 2 * deep, step, 0)
+
+    def block(e, k):
+        return pv.at[pl.ds(pl.multiple_of((2 * e + y) * rows, 16), rows), cut(k)]
+
+    def y_send(k, e):
+        src = pv.at[pl.ds(pl.multiple_of((2 * e + 1 - y) * rows, 16), rows), cut(k)]
+        return send(src, lines(yb, e).at[:, cut(k)], sy.at[k, e], ry.at[k, e], side)
+
+    def y_start(k):
+        for e in range(deep):
+            y_send(k, e).start()
+
+    def y_add(k):
+        for e in range(deep):
+            y_send(k, e).wait_recv()
+            add_into(block(e, k), lines(yb, e).at[:, cut(k)])
+
+    def z_send(k, e, slot, sem, who):
+        return send(block(e, k), lines(zb, slot).at[:, cut(k)], sem.at[k, e], rz.at[k, slot], who)
+
+    def hop(k, h):
+        @pl.when(z == h - 1)
+        def _():
+            for e in range(top, h - 1, -1):
+                if h > 1:
+                    z_send(k, e, e, su, up).wait_recv()
+                    add_into(block(e, k), lines(zb, e).at[:, cut(k)])
+                z_send(k, e, e, su, up).start()
+
+        @pl.when(z == deep - h)
+        def _():
+            for e in range(deep - h):
+                if h > 1:
+                    z_send(k, e, e, sd, down).wait_recv()
+                    add_into(block(e, k), lines(zb, e).at[:, cut(k)])
+                z_send(k, e, deep if e == deep - h - 1 else e, sd, down).start()
+
+    def g_spot(who, k):
+        return gath.at[who, :, cut(k)]
+
+    def finish(k):
+        mine = block(z, k)
+
+        @pl.when(z > 0)
+        def _():
+            z_send(k, z, z, su, up).wait_recv()
+            add_into(mine, lines(zb, z).at[:, cut(k)])
+
+        @pl.when(z < top)
+        def _():
+            z_send(k, z, deep, sd, down).wait_recv()
+            add_into(mine, lines(zb, deep).at[:, cut(k)])
+
+        send(mine, g_spot(s, k), gx_s.at[k], gx_r.at[k], across).start()
+        send(mine, g_spot(s, k), gc_s.at[0, k], gc_r.at[0, k], twin).start()
+        pltpu.make_async_copy(mine, g_spot(s, k), loc.at[3 + k]).start()
+
+    def spread(k):
+        spot = g_spot(across[1], k)
+        send(spot, spot, gx_s.at[k], gx_r.at[k], across).wait_recv()
+        send(spot, spot, gc_s.at[1, k], gc_r.at[1, k], twin).start()
+
+    half = gw.shape[0] // 2
+    lump = half // LUMPS
+
+    def w_rows(col, i):
+        return gw.at[pl.ds(pl.multiple_of(col * half + i * lump, 16), lump)]
+
+    def piece(ref, i):
+        return ref.at[pl.ds(i * lump, lump)]
+
+    def wy_send(i):
+        return send(w_rows(1 - y, i), piece(ybw, i), wy_s.at[i], wy_r.at[i], side)
+
+    def w_compute():
+        tall = 128
+
+        def step(i, _):
+            at = pl.ds(pl.multiple_of(i * tall, 16), tall)
+            for j in range(0, cot_v.shape[1], 512):
+                gw[at, j : j + 512] = mm(st_v[at, :], cot_v[:, j : j + 512]).astype(BF16)
+            return 0
+
+        lax.fori_loop(0, gw.shape[0] // tall, step, 0)
+        for i in range(LUMPS):
+            wy_send(i).start()
+
+    def from_below(i):
+        return send(w_rows(y, i), piece(zbw.at[0], i), wu_s.at[i], wz_r.at[0, i], up)
+
+    def from_above(i):
+        return send(w_rows(y, i), piece(zbw.at[1], i), wd_s.at[i], wz_r.at[1, i], down)
+
+    def w_cast(i, who, ssem, rsem):
+        return send(piece(wof, i), piece(wof, i), ssem.at[i], rsem.at[i], who)
+
+    root = z == s
+
+    def w_chain(i):
+        wy_send(i).wait_recv()
+        add_into(w_rows(y, i), piece(ybw, i))
+
+        @pl.when((z <= s) & (z > 0))
+        def _():
+            from_below(i).wait_recv()
+            add_into(w_rows(y, i), piece(zbw.at[0], i))
+
+        @pl.when((z >= s) & (z < top))
+        def _():
+            from_above(i).wait_recv()
+            add_into(w_rows(y, i), piece(zbw.at[1], i))
+
+        @pl.when(z < s)
+        def _():
+            from_below(i).start()
+
+        @pl.when(z > s)
+        def _():
+            from_above(i).start()
+
+        @pl.when(root)
+        def _():
+            piece(wof, i)[...] = w_rows(y, i)[...]
+            w_cast(i, across, bx_s, bx_r).start()
+            w_cast(i, twin, bc_s, bc_r).start()
+
+    def w_spread(i):
+        @pl.when(across[1] == z)
+        def _():
+            w_cast(i, across, bx_s, bx_r).wait_recv()
+            w_cast(i, twin, bc_s, bc_r).start()
+
+        @pl.when((across[1] != z) & jnp.logical_not(root))
+        def _():
+            w_cast(i, twin, bc_s, bc_r).wait_recv()
+
+    loads[0].wait()
+    for t in range(PARTS):
+        loads[1 + t].wait()
+        weigh(t)
+        y_start(t)
+        if t == 0:
+            x_start(0, outp)
+            x_start(1, ngp)
+        if t > 0:
+            y_add(t - 1)
+        for h in range(1, deep):
+            if t - h >= 0:
+                hop(t - h, h)
+        if t - deep >= 0:
+            finish(t - deep)
+    loads[1 + PARTS].wait()
+    loads[2 + PARTS].wait()
+    w_compute()
+    pair_sum(0, outp, 1)
+    pair_sum(1, ngp, 1)
+    for t in range(PARTS, PARTS + deep + 1):
+        if t == PARTS:
+            y_add(t - 1)
+        for h in range(1, deep):
+            if 0 <= t - h < PARTS:
+                hop(t - h, h)
+        if 0 <= t - deep < PARTS:
+            finish(t - deep)
+        if 0 <= t - deep - 1 < PARTS:
+            spread(t - deep - 1)
+    x_finish(0, out_o)
+    for i in range(LUMPS):
+        w_chain(i)
+    x_finish(1, ng_o)
+    for i in range(LUMPS):
+        w_spread(i)
+    wo_copy = pltpu.make_async_copy(wof, wo_o, out.at[1])
+    wo_copy.start()
+    for k in range(PARTS):
+        for n in range(2):
+            spot = g_spot(twin[1], k)
+            send(spot, spot, gc_s.at[n, k], gc_r.at[n, k], twin).wait_recv()
+        pltpu.make_async_copy(g_spot(s, k), g_spot(s, k), loc.at[3 + k]).wait()
+    gw_copy = pltpu.make_async_copy(gath, gw_o, out.at[0])
+    gw_copy.start()
+    for n, ref, dst in both:
+        for q in range(2):
+            for turn in range(2):
+                twin_send(n, ref, turn, q).wait_send()
+            x_send(n, q).wait_send()
+            pltpu.make_async_copy(xr.at[n, q], dst.at[q], out.at[2 + 2 * n + q]).wait()
+    for k in range(PARTS):
+        for e in range(deep):
+            y_send(k, e).wait_send()
+
+            @pl.when(z < e)
+            def _():
+                z_send(k, e, e, su, up).wait_send()
+
+            @pl.when(z > e)
+            def _():
+                z_send(k, e, e, sd, down).wait_send()
+
+        spot = g_spot(s, k)
+        send(spot, spot, gx_s.at[k], gx_r.at[k], across).wait_send()
+        for n in range(2):
+            send(spot, spot, gc_s.at[n, k], gc_r.at[n, k], twin).wait_send()
+    for i in range(LUMPS):
+        wy_send(i).wait_send()
+
+        @pl.when(z < s)
+        def _():
+            from_below(i).wait_send()
+
+        @pl.when(z > s)
+        def _():
+            from_above(i).wait_send()
+
+        @pl.when(root)
+        def _():
+            w_cast(i, across, bx_s, bx_r).wait_send()
+
+        @pl.when(root | (across[1] == z))
+        def _():
+            w_cast(i, twin, bc_s, bc_r).wait_send()
+
+    wo_copy.wait()
+    gw_copy.wait()
+
+
+def scatter(normed_t, pg, scaled_t, cot, outp, ngp, shards, groups):
+    model, count = normed_t.shape
+    total = pg.shape[1]
+    inner = scaled_t.shape[0]
+    seqs, length, _ = outp.shape
+    part = length // groups
+    deep = shards // 2
+    rows = model // shards
+    any_ = pl.BlockSpec(memory_space=pl.ANY)
+    dma = pltpu.SemaphoreType.DMA
+    v = pltpu.VMEM
+    return pl.pallas_call(
+        functools.partial(scatter_kernel, (deep, rows, part)),
+        in_specs=[any_] * 6,
+        out_specs=[any_] * 4,
+        out_shape=[
+            jax.ShapeDtypeStruct((groups, rows, total), BF16),
+            jax.ShapeDtypeStruct((inner // 2, model), BF16),
+            jax.ShapeDtypeStruct((seqs, part, model), BF16),
+            jax.ShapeDtypeStruct((seqs, part, model), BF16),
+        ],
+        scratch_shapes=[
+            v((model, count), BF16),
+            v((count, total), BF16),
+            v((inner, count), BF16),
+            v((count, model), BF16),
+            v((model, total), BF16),
+            v((deep * rows, total), BF16),
+            v(((deep + 1) * rows, total), BF16),
+            v((groups, rows, total), BF16),
+            v((2, 2, 2, part, model), BF16),
+            v((2, 2, part, model), BF16),
+            v((2, part, model), BF16),
+            v((inner, model), BF16),
+            v((inner // 2, model), BF16),
+            v((2, inner // 2, model), BF16),
+            v((inner // 2, model), BF16),
+            dma((PARTS, deep)), dma((PARTS, deep)), dma((PARTS, deep)), dma((PARTS, deep)),
+            dma((PARTS, deep + 1)),
+            dma((PARTS,)), dma((PARTS,)), dma((2, PARTS)), dma((2, PARTS)),
+            dma((2, 2, 2)), dma((2, 2, 2)), dma((2, 2)), dma((2, 2)),
+            dma((LUMPS,)), dma((LUMPS,)), dma((LUMPS,)), dma((LUMPS,)), dma((2, LUMPS)),
+            dma((LUMPS,)), dma((LUMPS,)), dma((LUMPS,)), dma((LUMPS,)),
+            dma((3 + PARTS,)), dma((2,)), dma((6,)),
+        ],
+        compiler_params=pltpu.CompilerParams(
+            collective_id=2, has_side_effects=True, vmem_limit_bytes=60 * 2**20
+        ),
+        name="weigh_scatter",
+    )(normed_t, pg, scaled_t, cot, outp, ngp)
 
 
 def local(
@@ -749,6 +1221,7 @@
     owner = lax.axis_index("dp")
     seqs, part, model = tokens.shape
     length = part * groups
+    rows_in = w_in.shape[0]
     rows_out = w_out.shape[0]
     wide = rows_out * shards
     heads = dt_bias.shape[0]
@@ -761,6 +1234,14 @@
     channels = wide + state2
     share = channels // shards
     ratio = shards // groups
+    small_slice = groups == 4 and shards == 8
+
+    def own(a):
+        return lax.dynamic_slice_in_dim(a, place * inner, inner, 0)
+
+    def own_heads(a):
+        return lax.dynamic_slice_in_dim(a, place * mine, mine, 0)
+
     step_cols = jnp.pad(
         lax.dynamic_slice_in_dim(w_in, 2 * wide + state2 + place * mine, mine, 1),
         ((0, 0), (0, 128 - mine)),
@@ -786,8 +1267,8 @@
     floats = tokens.astype(F32)
     inverse = lax.rsqrt(jnp.mean(floats * floats, axis=-1, keepdims=True) + EPSILON)
     unit = floats * inverse
-    if shards == 8 and groups == 4:
-        normed, cot, pj, sg, w_full, wo, small_all = gather(
+    if small_slice:
+        turned, cot, pj, sg, w_full, wo, small_all = gather(
             w_mine, w_out, small, tokens, cotangent, shards, groups
         )
     else:
@@ -800,11 +1281,11 @@
     def unpack(i, count):
         return small_all[:, cut[i] : cut[i + 1]].reshape(shards, -1)[:, :count].reshape(-1)
 
-    norm_all = unpack(0, norm_gain.shape[0])
+    norm_all = unpack(0, rows_in)
     conv_b = unpack(1, share)
     gain_all = unpack(2, rows_out)
     conv_w = unpack(3, share * taps).reshape(channels, taps)
-    if not (shards == 8 and groups == 4):
+    if not small_slice:
         normed = lax.all_gather((unit * norm_all).astype(BF16), "seq", axis=1, tiled=True)
         cot = lax.all_gather(cotangent, "seq", axis=1, tiled=True)
         w_full = lax.all_gather(w_mine, "dp", axis=0, tiled=True)
@@ -816,12 +1297,6 @@
         wo = lax.psum(held, "dp")
         sg = jnp.einsum("std,cd->stc", cot, wo, preferred_element_type=F32).astype(BF16)
         pj = jnp.einsum("std,de->ste", normed, w_full, preferred_element_type=F32).astype(BF16)
-
-    def own(a):
-        return lax.dynamic_slice_in_dim(a, place * inner, inner, 0)
-
-    def own_heads(a):
-        return lax.dynamic_slice_in_dim(a, place * mine, mine, 0)
 
     def pad(v):
         return jnp.pad(v, (0, 128 - mine))
@@ -839,44 +1314,15 @@
         ]
     )
     cols = columns(segment_ids)
-    pre, ys, gn, st, red = mix_forward(pj, cols, sg, hp, ch)
-    totals = lax.psum(red[:, :2], "seq")
-    rho = lax.rsqrt(totals[:, 0] / wide + EPSILON)
-    k2 = rho**3 * totals[:, 1] / wide
-    cols2 = jnp.pad(jnp.stack([rho, k2], axis=-1), ((0, 0), (0, 0), (0, 126)))
-    product = jnp.einsum("stc,cd->std", gn, wo, preferred_element_type=F32)
-    product = (product * rho[:, :, None]).astype(BF16)
-    result = (
-        floats
-        + lax.psum_scatter(product, "seq", scatter_dimension=1, tiled=True).astype(F32)
-    ).astype(BF16)
-    cot_rho = (cot.astype(F32) * rho[:, :, None]).astype(BF16)
-    wo_grad = jnp.einsum("stc,std->cd", gn, cot_rho, preferred_element_type=F32).astype(BF16)
-    wo_grad = lax.psum(wo_grad, "dp").reshape(ratio, rows_out, model)
-    wo_grad = lax.dynamic_index_in_dim(wo_grad, owner % ratio, 0, False)
-    wo_grad = lax.psum(jnp.where(owner // ratio == place, wo_grad, jnp.zeros((), BF16)), "seq")
-    pg, chacc, hacc = mix_backward(
-        pj, cols, cols2, sg, pre, ys, st, hp, ch, selectors(inner // 128)
-    )
-    win_grad = jnp.einsum("std,ste->de", normed, pg, preferred_element_type=F32).astype(BF16)
-    win_grad = lax.psum_scatter(win_grad, "dp", scatter_dimension=0, tiled=True)
-    win_grad = lax.all_gather(win_grad, "seq", axis=0, tiled=False).astype(F32)
-    rows_in = win_grad.shape[1]
-    w_in_grad = jnp.concatenate(
-        [
-            win_grad[:, :, :span].transpose(1, 0, 2).reshape(rows_in, 2 * wide),
-            jnp.sum(win_grad[:, :, span : span + state2], axis=0),
-            win_grad[:, :, span + state2 : span + state2 + mine]
-            .transpose(1, 0, 2)
-            .reshape(rows_in, heads),
-        ],
-        axis=1,
-    )
-    ngrad = jnp.einsum("ste,de->std", pg, w_full, preferred_element_type=F32).astype(BF16)
-    ngrad = lax.psum_scatter(ngrad, "seq", scatter_dimension=1, tiled=True).astype(F32)
-    unit_grad = ngrad * norm_all
-    tokens_grad = cotangent.astype(F32) + inverse * (
-        unit_grad - unit * jnp.mean(unit_grad * unit, axis=-1, keepdims=True)
+    pre, ys, st, red = mix_forward(pj, cols, sg, hp, ch)
+    if small_slice:
+        rk = norms(red, wide, groups)
+    else:
+        totals = lax.psum(red[:, :2], "seq")
+        rho = lax.rsqrt(totals[:, 0] / wide + EPSILON)
+        rk = jnp.stack([rho, rho**3 * totals[:, 1] / wide] + [jnp.zeros_like(rho)] * 6, axis=1)
+    pg, chacc, hacc, scaled_t, outp, ngp = mix_backward(
+        pj, cols, rk, sg, pre, ys, st, hp, ch, selectors(inner // 128), wo, w_full
     )
     chsum = jnp.sum(chacc, axis=1)
     hsum = jnp.sum(hacc, axis=1)[:, :mine]
@@ -889,27 +1335,56 @@
     chan = jnp.concatenate(
         [spread(chsum[:, :inner], wide, place * inner), chsum[:, inner:]], axis=1
     )
-    packed = jnp.concatenate(
+    packed = jnp.concatenate([chan.reshape(-1), spread(hsum, heads, place * mine).reshape(-1)])
+    packed = lax.psum(packed, ("dp", "seq"))
+    if small_slice:
+        win_grad, wo_grad, out_sum, ngrad = scatter(
+            turned,
+            pg.reshape(seqs * length, -1),
+            scaled_t,
+            cot.reshape(seqs * length, -1),
+            outp,
+            ngp,
+            shards,
+            groups,
+        )
+    else:
+        win_grad = jnp.einsum("std,ste->de", normed, pg, preferred_element_type=F32)
+        win_grad = lax.psum_scatter(win_grad.astype(BF16), "dp", scatter_dimension=0, tiled=True)
+        win_grad = lax.all_gather(win_grad, "seq", axis=0, tiled=False)
+        wo_grad = jnp.dot(scaled_t, cot.reshape(seqs * length, -1), preferred_element_type=F32)
+        wo_grad = lax.psum(wo_grad.astype(BF16), "dp").reshape(ratio, rows_out, model)
+        wo_grad = lax.dynamic_index_in_dim(wo_grad, owner % ratio, 0, False)
+        wo_grad = lax.psum(
+            jnp.where(owner // ratio == place, wo_grad, jnp.zeros((), BF16)), "seq"
+        )
+        out_sum = lax.psum_scatter(outp, "seq", scatter_dimension=1, tiled=True)
+        ngrad = lax.psum_scatter(ngp, "seq", scatter_dimension=1, tiled=True)
+    win_grad = win_grad.astype(F32)
+    wo_grad = wo_grad.astype(F32)
+    w_in_grad = jnp.concatenate(
         [
-            chan[: taps + 1].reshape(-1),
-            chan[taps + 1, :wide],
-            jnp.sum(ngrad * unit, axis=(0, 1)),
-            spread(hsum, heads, place * mine).reshape(-1),
-        ]
+            *[win_grad[g, :, :span] for g in range(groups)],
+            jnp.sum(win_grad[:, :, span : span + state2], axis=0),
+            *[win_grad[g, :, span + state2 : span + state2 + mine] for g in range(groups)],
+        ],
+        axis=1,
     )
-    packed = lax.psum(packed, ("dp", "seq"))
+    norm_grad = jnp.sum(w_in.astype(F32) * w_in_grad, axis=1) / norm_gain.astype(F32)
+    gain_grad = jnp.sum(w_out.astype(F32) * wo_grad, axis=1) / gated_gain.astype(F32)
+    result = (floats + out_sum.astype(F32)).astype(BF16)
+    unit_grad = ngrad.astype(F32) * norm_all
+    tokens_grad = cotangent.astype(F32) + inverse * (
+        unit_grad - unit * jnp.mean(unit_grad * unit, axis=-1, keepdims=True)
+    )
     chan = packed[: (taps + 1) * channels].reshape(taps + 1, channels)
     chan = lax.dynamic_slice_in_dim(chan, owner * share, share, 1)
     at = (taps + 1) * channels
-    gain_grad = lax.dynamic_slice_in_dim(packed[at : at + wide], owner * rows_out, rows_out, 0)
-    at += wide
-    norm_grad = lax.dynamic_slice_in_dim(packed[at : at + model], owner * rows_in, rows_in, 0)
-    at += model
     return (
         result,
         tokens_grad,
         w_in_grad,
-        wo_grad.astype(F32),
+        wo_grad,
         chan[:taps].T,
         chan[taps],
         norm_grad,

time: 705 us -> 437 us (0.62)
  waiting for transfers between devices: 385 us -> 0.02 us
  Pallas kernels: 183 us -> 376 us
  matrix products: 54.3 us -> 0 us
  blocking collectives: 9.44 us -> 0 us
  other arithmetic: 25.4 us -> 18.2 us
    reduce_scatter x3 -> x0, waiting for transfers between devices: 172 us -> none  [the longest x1 113 us: local(): win_grad = lax.psum_scatter(win_grad, 'dp', scatter_dimension=0, tiled=True)]
    pallas_call x0 -> x2, Pallas kernels: none -> 155 us  [the longest x1 147 us: scatter(): pl.pallas_call(functools.partial(scatter_kernel, (deep, rows, part)), in_...]
    psum x1, waiting for transfers between devices: 123 us -> 0.01 us  [local(): packed = lax.psum(packed, ('dp', 'seq'))]
    psum x2 -> x0, waiting for transfers between devices: 67.6 us -> none  [the longest x1 39.4 us: local(): lax.psum(jnp.where(owner // ratio == place, wo_grad, jnp.zeros((), BF16))...]
    dot_general x4 -> x0, matrix products: 54.3 us -> none  [the longest x1 19.1 us: local(): jnp.einsum('std,ste->de', normed, pg, preferred_element_type=F32)]
    pallas_call x1, Pallas kernels: 45 us -> 80.5 us  [mix_backward(): pl.pallas_call(functools.partial(bwd_kernel, pairs), grid=(seqs, chunks),...]
    all_gather x1 -> x0, waiting for transfers between devices: 23.1 us -> none  [local(): win_grad = lax.all_gather(win_grad, 'seq', axis=0, tiled=False).astype(F32)]
    psum x1 -> x0, blocking collectives: 9.44 us -> none  [local(): totals = lax.psum(red[:, :2], 'seq')]
  transfers between devices with their start and end apart: 7 -> 1, of which waited for: 7 -> 0; matrix products, arithmetic and copies ran while one was open for 10% -> 5% of each run, Pallas kernels for 6% -> 34%
where the time goes in v3:
time: 437 us; the launch traced here: 436 us
  Pallas kernels  376 us (86%)
  local copies, waits for them, and re-layouts  27.2 us (6%)
  other arithmetic  18.2 us (4%)
  between operations  14.5 us (3%)
    pallas_call x1, Pallas kernels, scatter(): pl.pallas_call(functools.partial(scatter_kernel, (deep, rows, part)), in_...  147 us
    pallas_call x1, Pallas kernels, gather(): pl.pallas_call(functools.partial(gather_kernel, (deep, pieces, rows, inne...  115 us
    pallas_call x1, Pallas kernels, mix_backward(): pl.pallas_call(functools.partial(bwd_kernel, pairs), grid=(seqs, chunks),...  80.5 us
    pallas_call x1, Pallas kernels, mix_forward(): pl.pallas_call(functools.partial(fwd_kernel, pairs), grid=(seqs, chunks),...  24.9 us
  transfers between devices with their start and end apart: 1, of which 0 were waited for; matrix products, arithmetic and copies ran while one was open for 5% of the time, Pallas kernels for 34%

profile of v3, /device:TPU:3, one launch (start us, length us, event | category | flops | bytes accessed | tf_op | source)
XLA Modules:
  0.0 435.7 jit_solution(13066103808363548612)
XLA Ops:
  7.2 0.9 slice.117
  8.1 0.9 constant_dynamic-slice_fusion.1
  9.0 1.3 constant_dynamic-slice_fusion.2
  10.4 0.9 copy.46
  11.4 0.7 pad.70
  12.1 0.7 pad.71
  12.8 0.7 pad.69
  13.5 0.9 fusion.9.wm
  15.0 115.2 %gather_project.1 = (bf16[1536,2048]{1,0:T(8,128)(2,1)}, bf16[2,1024,1536]{2,1,0:T(8,128)(2,1)}, bf16[2,1024,1920]{2,1,0:T(8,128)(2,1)}, bf16[2,1024,768]{2,1,0:...) custom-call(bf16[192,1920]{1,0:T(8,128)(2,1)} %fusion.9.wm, ...), custom_call_target="tpu_custom_call" | custom-call | tf_op jit(solution)/shard_map/gather_project/pallas_call | solution.py:777
  130.3 0.9 convert_element_type.91
  131.4 1.7 reshape_reshape.3
  135.5 24.9 %mix_forward.1 = (f32[2,1024,1024]{2,1,0:T(8,128)}, f32[2,1024,768]{2,1,0:T(8,128)}, bf16[2,8,128,768]{3,2,1,0:T(8,128)(2,1)S(1)}, f32[2,8,1024]{2,1,0:T(8,128)S(1)}) custom-call(bf16[2,1024,1920]{2,1,0:T(8,128)(2,1)} %get-tuple-element.33.pj, f32[2,1024,128]{2,1,0:T(8,128)S(1)} %pad.81.cols, bf16[2,1024,768]{2,1,0:T(8,128)(2,1)} %get-tuple-element.34.sg, ...), custom_call_target="tpu_custom_call" | custom-call | tf_op jit(solution)/shard_map/mix_forward/pallas_call | solution.py:132
  160.4 1.7 copy-done
  162.6 8.2 %norms.1.rk = f32[2,8,1024]{2,1,0:T(8,128)} custom-call(f32[2,8,1024]{2,1,0:T(8,128)} %copy-done.4), custom_call_target="tpu_custom_call" | custom-call | tf_op jit(solution)/shard_map/norms/pallas_call | solution.py:419
  171.0 0.8 copy-done.2
  171.8 80.5 %mix_backward.1 = (bf16[2,1024,1920]{2,1,0:T(8,128)(2,1)}, f32[5,8,1024]{2,1,0:T(8,128)S(1)}, f32[3,8,128]{2,1,0:T(8,128)S(1)}, bf16[768,2048]{1,0:T(8,128)(2,1)...) custom-call(bf16[2,1024,1920]{2,1,0:T(8,128)(2,1)} %get-tuple-element.33.pj, ...), custom_call_target="tpu_custom_call" | custom-call | tf_op jit(solution)/shard_map/mix_backward/pallas_call | solution.py:323
  252.3 0.7 copy-done.3
  253.0 1.0 reduce_sum.66
  254.4 0.6 pad_maximum_fusion.1
  255.1 146.9 %weigh_scatter.1 = (bf16[4,192,1920]{2,1,0:T(8,128)(2,1)}, bf16[384,1536]{1,0:T(8,128)(2,1)}, bf16[2,256,1536]{2,1,0:T(8,128)(2,1)}, bf16[2,256,1536]{2,1,0:T(8,128)(2,1)}) custom-call(bf16[1536,2048]{1,0:T(8,128)(2,1)} %get-tuple-element.32.nt_in, bf16[2048,1920]{1,0:T(8,128)(2,1)} %bitcast.82, bf16[768,2048]{1,0:T(8,128)(2,1)} %get-tuple-element.43.st_in, ...), custom_call_target="tpu_custom_call" | custom-call | tf_op jit(solution)/shard_map/weigh_scatter/pallas_call | solution.py:1163
  402.0 2.2 convert_element_type.97
  404.3 2.0 slice_bitcast_fusion
  406.4 0.8 slice.163
  407.5 5.7 %concatenate.37 = f32[192,6448]{1,0:T(8,128)} concatenate(f32[192,1536]{1,0:T(8,128)} %get-tuple-element.64, f32[192,1536]{1,0:T(8,128)} %get-tuple-element.63, f32[192,1536]{1,0:T(8,128)} %get-tuple-element.62, f32[192,1536]{1,0:T(8,128)S(1)} %get-tuple-element.61, f32[192,256]{1,0:T(8,128)S(1)} %slice_reduce_fusion, f32[192,12]{1,0:T(8,128)S(1)} %get-tuple-element.60, ...), dimensions={1} | concatenate | bytes 9904128 | tf_op jit(solution)/shard_map/concatenate | solution.py:1365
  413.2 3.9 multiply_reduce_fusion
  417.2 0.7 fusion.2
  418.8 1.7 multiply_reduce_fusion.1
  421.1 3.5 fusion.5
  425.2 0.9 reshape.116
  426.1 0.7 dynamic-slice_bitcast_fusion
  426.8 0.7 dynamic-slice.1
  427.5 1.4 fusion.21
  (114 shorter events, 7.0 us)
Async XLA Ops:
  7.2 418.1 %all-reduce.21.cloned.1.call-start = ((), (), s32[]{:S(2)}) async-start(), calls=%async_computation | async-start | bytes 139264 | tf_op jit(solution)/shard_map/psum | solution.py:1339
  15.0 118.2 %copy-start.11 = (s32[2,1024]{1,0:T(2,128)S(1)}, s32[2,1024]{1,0:T(2,128)}, u32[]{:S(2)}) copy-start(s32[2,1024]{1,0:T(2,128)} %param.13) | copy-start | bytes 24580
  130.2 3.5 copy-start.15
  130.3 3.8 copy-start.14
  130.3 3.9 copy-start.16
  135.5 35.5 %copy-start.1 = (bf16[768,1536]{1,0:T(8,128)(2,1)S(1)}, bf16[768,1536]{1,0:T(8,128)(2,1)}, u32[]{:S(2)}) copy-start(bf16[768,1536]{1,0:T(8,128)(2,1)} %get-tuple-element.40.wo) | copy-start | bytes 7077892
  160.3 1.7 copy-start
  162.0 0.6 copy-start.4
  171.0 0.8 copy-start.2
  252.3 0.7 copy-start.3
  404.2 2.9 copy-start.5
  413.2 4.0 copy-start.7
  417.2 1.3 copy-start.8
  417.2 1.6 copy-start.10
  418.0 2.6 copy-start.12
  418.0 3.1 copy-start.6
  418.0 3.1 copy-start.9
  421.1 3.5 copy-start.13
Sparse Core Ops, SparseCore 0:
  255.2 121.5 all-reduce.20
